TPU v7x, 512 devices: a whole 4x8x8 slice. The times are simulated.
512 devices in a mesh: grp: 4 (over x), dp: 16 (over y, core), tensor: 8 (over z).
Axes of the slice: x: 4, y: 8, z: 8, core: 2. Of those that a mesh axis runs over, the one named last changes fastest.
Arguments:
- queries: bfloat16 [512, 64, 576], P(('grp', 'dp'), 'tensor'), may hold values from -1006 to 1006
- latent_cache: bfloat16 [512, 128, 576], P(('grp', 'dp')), may hold values from -4 to 4
- lengths: int32 [512], P(('grp', 'dp')), may hold values from 2 to 128, as said below
- value_up: bfloat16 [64, 512, 128], P('tensor'), may hold values from -0.25 to 0.25
- out_proj: bfloat16 [8192, 7168], P('tensor', 'dp'), may hold values from -0.1875 to 0.1875
- residual_in: bfloat16 [512, 7168], P(('grp', 'tensor'), 'dp'), may hold values from -12 to 12
- norm_gain: bfloat16 [7168], P('dp'), may hold values from 0.099609375 to 1.8984375
- router: bfloat16 [16, 7168], P('grp', 'dp'), may hold values from -0.0625 to 0.0625
- gate_up: bfloat16 [16, 7168, 2, 1024], P('grp', 'dp', None, 'tensor'), may hold values from -0.0625 to 0.0625
- down_proj: bfloat16 [16, 1024, 7168], P('grp', 'tensor', 'dp'), may hold values from -0.5 to 0.5
- routes: int32 [512, 8], P(('grp', 'tensor')), may hold values from 0 to 15, all different within a row; in each aligned block of 16 rows (0 to 15, 16 to 31, ...) at most 12 rows name the same one
- expert_slot: int32 [16], replicated, may hold values from 0 to 15, each once
Outputs:
- layer_out: bfloat16 [512, 7168], P(('grp', 'tensor'), 'dp')
Inputs may be any that keep to these rules, and one draw needn't show every extreme that they name: `routes`: each row names 8 different experts; within each aligned block of 16 rows (the rows of one device) no expert is named by more than 12 rows, and some block reaches it. `expert_slot`: a permutation. `lengths`: some sequence uses all 128 positions.
All inputs are finite; a program needn't handle non-finite values.
Results may differ from a plain program's by a relative error of at most 0.012.
Values may be sent and summed in bfloat16 or wider, within the bound.
A program may use at most 64 MiB of HBM per device.

v0:
```python
import jax
import jax.numpy as jnp
from jax import lax
from jax.sharding import PartitionSpec as P

D = 7168
ROPE = 64
VHEAD = 128


EPSILON = 1e-06


def on_device(
    queries,
    latent_cache,
    lengths,
    value_up,
    out_proj,
    residual_in,
    norm_gain,
    router,
    gate_up,
    down_proj,
    routes,
    expert_slot,
):
    seq_rows = queries.shape[0]
    head_count = queries.shape[1]
    cache_len = latent_cache.shape[1]
    latent_dim = value_up.shape[1]
    score_scale = (VHEAD + ROPE) ** (-0.5)
    scores = (
        jnp.einsum("nhc,njc->nhj", queries, latent_cache, preferred_element_type=jnp.float32)
        * score_scale
    )
    positions = lax.broadcasted_iota(jnp.int32, (1, 1, cache_len), 2)
    scores = jnp.where(positions < lengths[:, None, None], scores, -1e30)
    row_max = jnp.max(scores, axis=2, keepdims=True)
    weights = jnp.exp(scores - row_max)
    prob_rows = (weights / jnp.sum(weights, axis=2, keepdims=True)).astype(jnp.bfloat16)
    latent = jnp.einsum(
        "nhj,njc->nhc",
        prob_rows,
        latent_cache[:, :, :latent_dim],
        preferred_element_type=jnp.float32,
    ).astype(jnp.bfloat16)
    head_out = jnp.einsum(
        "nhc,hcv->nhv", latent, value_up, preferred_element_type=jnp.float32
    ).astype(jnp.bfloat16)
    head_out = head_out.reshape(seq_rows, head_count * value_up.shape[2])
    gathered = lax.all_gather(head_out, "dp", axis=0, tiled=True)
    token_rows = residual_in.shape[0]
    attn_out = lax.psum_scatter(
        jnp.dot(gathered, out_proj, preferred_element_type=jnp.float32),
        "tensor",
        scatter_dimension=0,
        tiled=True,
    )
    stream = (residual_in.astype(jnp.float32) + attn_out).astype(jnp.bfloat16)
    expert_count = expert_slot.shape[0]
    top_count = routes.shape[1]
    local_experts = gate_up.shape[0]
    col_width = stream.shape[1]
    capacity = 3 * token_rows // 4
    group_count = lax.axis_size("grp")
    tensor_count = lax.axis_size("tensor")
    slot_width = local_experts * capacity
    expert_ids = lax.broadcasted_iota(jnp.int32, (1, 1, expert_count), 2)
    id_hot = (routes[:, :, None] == expert_ids).astype(jnp.int32)
    slot_of = jnp.sum(id_hot * expert_slot[None, None, :], axis=2)
    slot_hot = (slot_of.reshape(-1, 1) == expert_ids.reshape(1, expert_count)).astype(jnp.int32)
    earlier = jnp.cumsum(slot_hot, axis=0) - slot_hot
    position = jnp.sum(earlier * slot_hot, axis=1)
    slot_index = (slot_of.reshape(-1) * capacity + position).reshape(token_rows, top_count)
    slot_ids = lax.broadcasted_iota(jnp.int32, (expert_count * capacity, 1, 1), 0)
    mapping = jnp.sum((slot_index[None, :, :] == slot_ids).astype(jnp.float32), axis=2)
    outgoing = jnp.dot(
        mapping.astype(jnp.bfloat16), stream, preferred_element_type=jnp.float32
    ).astype(jnp.bfloat16)
    outgoing = outgoing.reshape(group_count, 1, slot_width, col_width)
    copies = jnp.broadcast_to(outgoing, (group_count, tensor_count, slot_width, col_width))
    copies = copies.reshape(group_count * tensor_count, slot_width, col_width)
    arrived = lax.all_to_all(copies, ("grp", "tensor"), split_axis=0, concat_axis=0, tiled=True)
    slot_rows = arrived.reshape(group_count * tensor_count, local_experts, capacity, col_width)
    scaled = (slot_rows.astype(jnp.float32) * norm_gain.astype(jnp.float32)).astype(jnp.bfloat16)
    gate_up_sum = jnp.einsum(
        "secd,edkh->seckh", scaled, gate_up, preferred_element_type=jnp.float32
    )
    router_logit = jnp.einsum("secd,ed->sec", scaled, router, preferred_element_type=jnp.float32)
    squares = jnp.sum(jnp.square(slot_rows.astype(jnp.float32)), axis=3)
    gate_up_sum, router_logit, squares = lax.psum((gate_up_sum, router_logit, squares), "dp")
    inv_rms = lax.rsqrt(squares / D + EPSILON)
    gate_part = gate_up_sum[:, :, :, 0, :] * inv_rms[..., None]
    up_part = gate_up_sum[:, :, :, 1, :] * inv_rms[..., None]
    hidden = (jax.nn.silu(gate_part) * up_part).astype(jnp.bfloat16)
    down_part = jnp.einsum("sech,ehd->secd", hidden, down_proj, preferred_element_type=jnp.float32)
    router_score = jax.nn.sigmoid(router_logit * inv_rms)
    slot_term = (router_score[..., None] * down_part).reshape(
        group_count, tensor_count, slot_width, col_width
    )
    slot_share = (router_score / tensor_count).reshape(group_count, tensor_count, slot_width)
    flat_term = slot_term.reshape(group_count * tensor_count, slot_width, col_width)
    flat_share = slot_share.reshape(group_count * tensor_count, slot_width)
    returned, returned_share = (
        lax.all_to_all(flat_term, ("grp", "tensor"), split_axis=0, concat_axis=0, tiled=True),
        lax.all_to_all(flat_share, ("grp", "tensor"), split_axis=0, concat_axis=0, tiled=True),
    )
    summed_rows = jnp.sum(returned.reshape(group_count, -1, slot_width, col_width), axis=1).reshape(
        expert_count * capacity, col_width
    )
    summed_share = jnp.sum(returned_share.reshape(group_count, -1, slot_width), axis=1).reshape(
        expert_count * capacity
    )
    numerator = jnp.einsum("qr,qd->rd", mapping, summed_rows, precision=lax.Precision.HIGHEST)
    denominator = jnp.einsum("qr,q->r", mapping, summed_share, precision=lax.Precision.HIGHEST)
    moe = numerator / denominator[:, None]
    return (stream.astype(jnp.float32) + moe).astype(jnp.bfloat16)


def solution(mesh):
    in_specs = (
        P(("grp", "dp"), "tensor", None),
        P(("grp", "dp"), None, None),
        P(("grp", "dp")),
        P("tensor", None, None),
        P("tensor", "dp"),
        P(("grp", "tensor"), "dp"),
        P("dp"),
        P("grp", "dp"),
        P("grp", "dp", None, "tensor"),
        P("grp", "tensor", "dp"),
        P(("grp", "tensor"), None),
        P(),
    )
    out_specs = P(("grp", "tensor"), "dp")
    return jax.shard_map(
        on_device, mesh=mesh, in_specs=in_specs, out_specs=out_specs, check_vma=False
    )
```

profile of v0, /device:TPU:1, one launch (start us, length us, event | category | flops | bytes accessed | tf_op | source)
XLA Modules:
  0.0 334.3 jit_solution(12840982223636133547)
XLA Ops:
  6.5 0.0 copy-start
  6.5 0.0 reduce-scatter.2.cloned.1.call-start
  6.5 0.8 iota_compare_fusion.3
  7.4 1.6 fusion.8
  9.0 0.0 copy-start.3
  9.0 0.2 fusion.29
  9.1 1.7 convolution_convert_fusion.1
  10.8 0.0 copy-done
  10.9 0.0 copy-start.10
  10.9 0.0 copy-start.12
  10.9 0.0 copy-start.5
  10.9 0.2 fusion.11
  11.1 21.6 %all_gather.3 = bf16[128,1024]{1,0:T(8,128)(2,1)S(1)} all-gather(bf16[8,1024]{1,0:T(8,128)(2,1)S(1)} %fusion.11), channel_id=1, replica_groups=mesh['grp'=4,'dp'=16,'tensor'=8] {'dp'}, dimensions={0}, use_global_device_ids=true | all-gather | bytes 278528 | tf_op jit(solution)/shard_map/all_gather | solution.py:52
  32.7 0.0 copy-done.3
  32.7 1.1 fusion.30
  33.8 0.0 reduce-scatter.2.cloned.1.call-update
  33.9 0.0 copy-done.10
  33.9 0.1 copy.43
  34.0 0.0 copy-done.12
  34.0 0.4 select_reduce_fusion.1
  34.4 0.1 eq.44
  34.5 0.1 fusion.24
  34.6 0.2 reduce_window_sum.11
  34.7 0.2 select_reduce_fusion
  34.9 0.1 reduce_sum.70
  35.0 0.1 convert_reduce_fusion
  35.1 33.1 %reduce-scatter.2.cloned.1.call-done = f32[16,448]{1,0:T(8,128)} async-done(((f32[128,448]{1,0:T(8,128)}), f32[16,448]{1,0:T(8,128)}) %reduce-scatter.2.cloned.1.call-update) | async-done | bytes 28688 | tf_op jit(solution)/shard_map/reduce_scatter | solution.py:54
  68.2 0.0 copy-done.5
  68.2 1.0 convolution_convert_fusion
  69.2 1.3 broadcast_in_dim.19
  70.6 7.6 %all-to-all-start = ((bf16[32,48,448]{2,1,0:T(8,128)(2,1)}), bf16[32,48,448]{2,1,0:T(8,128)(2,1)S(1)}, u32[]{:S(2)}, u32[]{:S(2)}) async-start(bf16[32,48,448]{2,1,0:T(8,128)(2,1)} %bitcast.72), calls=%async_computation.1 | async-start | bytes 3145728 | tf_op jit(solution)/shard_map/all_to_all | solution.py:84
  78.2 0.0 all-reduce.3.cloned.1.call-start
  78.2 0.0 copy-done.11
  78.2 0.6 convert_element_type.69
  78.8 29.1 %all-to-all-done = bf16[32,48,448]{2,1,0:T(8,128)(2,1)S(1)} async-done(((bf16[32,48,448]{2,1,0:T(8,128)(2,1)}), bf16[32,48,448]{2,1,0:T(8,128)(2,1)S(1)}, u32[]{:S(2)}, u32[]{:S(2)}) %all-to-all-start) | async-done | bytes 1376288 | tf_op jit(solution)/shard_map/all_to_all | solution.py:84
  107.9 0.9 copy_convert_fusion
  108.8 0.0 copy-start.1
  108.8 1.7 copy-done.1
  110.5 0.0 copy-done.2
  110.5 0.0 copy-done.7
  110.5 1.8 fusion.3
  112.3 0.0 all-reduce.3.cloned.1.call-update
  112.3 1.0 multiply_reduce_fusion
  113.2 0.0 copy-done.8
  113.2 0.0 copy-done.9
  113.2 0.0 copy-start.13
  113.3 2.5 fusion.18
  115.7 0.4 copy.52
  116.2 53.5 %all-reduce = (f32[32,4,12]{0,2,1:T(8,128)S(1)}, f32[32,4,12]{0,2,1:T(8,128)S(1)}) all-reduce(f32[32,4,12]{0,2,1:T(8,128)S(1)} %bitcast.77, f32[32,4,12]{0,2,1:T(8,128)S(1)} %reduce_sum.73), channel_id=1, replica_groups=mesh['grp'=4,'dp'=16,'tensor'=8] {'dp'}, use_global_device_ids=true, to_apply=%region_7.8 | all-reduce | flops 3072 | bytes 24576 | tf_op jit(solution)/shard_map/psum | solution.py:92
  169.7 0.7 copy.50
  170.4 4.8 %all-to-all-start.2 = ((f32[32,1,48]{2,1,0:T(1,128)}), f32[32,1,48]{2,1,0:T(1,128)S(1)}, u32[]{:S(2)}, u32[]{:S(2)}) async-start(f32[32,1,48]{2,1,0:T(1,128)} %copy.50), calls=%async_computation.3 | async-start | bytes 32768 | tf_op jit(solution)/shard_map/all_to_all | solution.py:107
  175.2 62.4 %all-reduce.3.cloned.1.call-done = f32[32,4,12,2,128]{4,0,3,2,1:T(8,128)} async-done(((f32[32,4,12,2,128]{4,0,3,2,1:T(8,128)}), f32[32,4,12,2,128]{4,0,3,2,1:T(8,128)}) %all-reduce.3.cloned.1.call-update) | async-done | bytes 1572880 | tf_op jit(solution)/shard_map/psum | solution.py:92
  237.6 0.0 copy-done.13
  237.6 2.1 bitcast_multiply_fusion
  239.6 3.5 %copy.47 = f32[32,48,448]{2,1,0:T(8,128)} copy(f32[32,48,448]{2,0,1:T(8,128)S(1)} %bitcast.73) | data formatting | bytes 5505024 | tf_op jit(solution)/shard_map/reshape;reshape | solution.py:103
  243.2 0.0 all-to-all-done.2
  243.2 10.0 %all-to-all-start.1 = ((f32[32,48,448]{2,1,0:T(8,128)}), f32[32,48,448]{2,1,0:T(8,128)}, u32[]{:S(2)}, u32[]{:S(2)}) async-start(f32[32,48,448]{2,1,0:T(8,128)} %copy.47), calls=%async_computation.2 | async-start | bytes 6291456 | tf_op jit(solution)/shard_map/all_to_all | solution.py:106
  253.2 0.1 reshape.80
  253.3 0.1 convolution_bitcast_fusion
  253.4 70.7 %all-to-all-done.1 = f32[32,48,448]{2,1,0:T(8,128)} async-done(((f32[32,48,448]{2,1,0:T(8,128)}), f32[32,48,448]{2,1,0:T(8,128)}, u32[]{:S(2)}, u32[]{:S(2)}) %all-to-all-start.1) | async-done | bytes 2752544 | tf_op jit(solution)/shard_map/all_to_all | solution.py:106
  324.2 2.3 bitcast_reduce_fusion
  326.5 0.0 copy-done.4
  326.5 0.0 copy-done.6
  326.5 0.9 fusion.10
  (12 shorter events, 0.1 us)
Async XLA Ops:
  6.5 4.3 %copy-start = (bf16[8,512,128]{2,1,0:T(8,128)(2,1)S(1)}, bf16[8,512,128]{2,1,0:T(8,128)(2,1)}, u32[]{:S(2)}) copy-start(bf16[8,512,128]{2,1,0:T(8,128)(2,1)} %param.15) | copy-start | bytes 3145732
  6.5 61.7 %reduce-scatter.2.cloned.1.call-start = ((), (), s32[]{:S(2)}) async-start(), calls=%async_computation.4 | async-start | bytes 294912 | tf_op jit(solution)/shard_map/reduce_scatter | solution.py:54
  9.0 23.8 %copy-start.3 = (bf16[1024,448]{0,1:T(8,128)(2,1)S(1)}, bf16[1024,448]{0,1:T(8,128)(2,1)}, u32[]{:S(2)}) copy-start(bf16[1024,448]{0,1:T(8,128)(2,1)} %param.16) | copy-start | bytes 2752516
  10.9 23.0 %copy-start.10 = (s32[16,8]{0,1:T(8,128)S(1)}, s32[16,8]{0,1:T(8,128)}, u32[]{:S(2)}) copy-start(s32[16,8]{0,1:T(8,128)} %param.22) | copy-start | bytes 1540
  10.9 23.1 %copy-start.12 = (s32[16]{0:T(128)S(1)}, s32[16]{0:T(128)}, u32[]{:S(2)}) copy-start(s32[16]{0:T(128)} %param.23) | copy-start | bytes 196
  10.9 57.4 %copy-start.5 = (bf16[16,448]{1,0:T(8,128)(2,1)S(1)}, bf16[16,448]{1,0:T(8,128)(2,1)}, u32[]{:S(2)}) copy-start(bf16[16,448]{1,0:T(8,128)(2,1)} %param.17) | copy-start | bytes 43012
  70.6 7.7 %copy-start.11 = (bf16[448]{0:T(512)(128)(2,1)S(1)}, bf16[448]{0:T(512)(128)(2,1)}, u32[]{:S(2)}) copy-start(bf16[448]{0:T(512)(128)(2,1)} %param.18) | copy-start | bytes 2692
  70.6 37.3 %all-to-all-start = ((bf16[32,48,448]{2,1,0:T(8,128)(2,1)}), bf16[32,48,448]{2,1,0:T(8,128)(2,1)S(1)}, u32[]{:S(2)}, u32[]{:S(2)}) async-start(bf16[32,48,448]{2,1,0:T(8,128)(2,1)} %bitcast.72), calls=%async_computation.1 | async-start | bytes 3145728 | tf_op jit(solution)/shard_map/all_to_all | solution.py:84
  78.2 159.4 %all-reduce.3.cloned.1.call-start = ((), (), s32[]{:S(2)}) async-start(), calls=%async_computation.5 | async-start | bytes 3145728 | tf_op jit(solution)/shard_map/psum | solution.py:92
  78.8 31.7 %copy-start.2 = (bf16[4,448,2,128]{3,2,1,0:T(2,128)(2,1)S(1)}, bf16[4,448,2,128]{3,2,1,0:T(2,128)(2,1)}, u32[]{:S(2)}) copy-start(bf16[4,448,2,128]{3,2,1,0:T(2,128)(2,1)} %param.20) | copy-start | bytes 2752516
  107.9 2.6 copy-start.7
  108.8 1.7 copy-start.1
  112.2 1.0 copy-start.8
  112.3 1.0 copy-start.9
  113.2 124.3 %copy-start.13 = (bf16[4,128,448]{1,2,0:T(8,128)(2,1)S(1)}, bf16[4,128,448]{1,2,0:T(8,128)(2,1)}, u32[]{:S(2)}) copy-start(bf16[4,128,448]{1,2,0:T(8,128)(2,1)} %param.21) | copy-start | bytes 1376260
  170.4 72.8 %all-to-all-start.2 = ((f32[32,1,48]{2,1,0:T(1,128)}), f32[32,1,48]{2,1,0:T(1,128)S(1)}, u32[]{:S(2)}, u32[]{:S(2)}) async-start(f32[32,1,48]{2,1,0:T(1,128)} %copy.50), calls=%async_computation.3 | async-start | bytes 32768 | tf_op jit(solution)/shard_map/all_to_all | solution.py:107
  243.2 81.0 %all-to-all-start.1 = ((f32[32,48,448]{2,1,0:T(8,128)}), f32[32,48,448]{2,1,0:T(8,128)}, u32[]{:S(2)}, u32[]{:S(2)}) async-start(f32[32,48,448]{2,1,0:T(8,128)} %copy.47), calls=%async_computation.2 | async-start | bytes 6291456 | tf_op jit(solution)/shard_map/all_to_all | solution.py:106
  253.4 73.1 %copy-start.4 = (f32[16,448]{1,0:T(8,128)S(1)}, f32[16,448]{1,0:T(8,128)}, u32[]{:S(2)}) copy-start(f32[16,448]{1,0:T(8,128)} %reduce-scatter.2.cloned.1.call-done) | copy-start | bytes 86020
  253.4 73.1 %copy-start.6 = (bf16[16,448]{1,0:T(8,128)(2,1)S(1)}, bf16[16,448]{1,0:T(8,128)(2,1)}, u32[]{:S(2)}) copy-start(bf16[16,448]{1,0:T(8,128)(2,1)} %param.17) | copy-start | bytes 43012
Sparse Core Ops, SparseCore 0:
  34.0 34.2 reduce-scatter.1
  112.4 125.1 all-reduce.2
where the time goes:
time: 337 us; the launch traced here: 334 us
  waiting for transfers between devices  195 us (58%)
  blocking collectives  75 us (22%)
  starting transfers between devices  22.4 us (7%)
  between operations  13.6 us (4%)
  matrix products  13.1 us (4%)
  local copies, waits for them, and re-layouts  8.03 us (2%)
  other arithmetic  6.75 us (2%)
    all_to_all x1, waiting for transfers between devices, on_device(): lax.all_to_all(flat_term, ('grp', 'tensor'), split_axis=0, concat_axis=0,...  70.7 us
    psum x1, waiting for transfers between devices, on_device(): lax.psum((gate_up_sum, router_logit, squares), 'dp')  62.4 us
    psum x1, blocking collectives, on_device(): lax.psum((gate_up_sum, router_logit, squares), 'dp')  53.5 us
    reduce_scatter x1, waiting for transfers between devices, on_device(): lax.psum_scatter(jnp.dot(gathered, out_proj, preferred_element_type=jnp.f...  33.1 us
    all_to_all x1, waiting for transfers between devices, on_device(): lax.all_to_all(copies, ('grp', 'tensor'), split_axis=0, concat_axis=0, ti...  29.1 us
    all_gather x1, blocking collectives, on_device(): gathered = lax.all_gather(head_out, 'dp', axis=0, tiled=True)  21.6 us
    all_to_all x1, starting transfers between devices, on_device(): lax.all_to_all(flat_term, ('grp', 'tensor'), split_axis=0, concat_axis=0,...  10 us
    all_to_all x1, starting transfers between devices, on_device(): lax.all_to_all(copies, ('grp', 'tensor'), split_axis=0, concat_axis=0, ti...  7.6 us
  transfers between devices with their start and end apart: 5, of which 4 were waited for; matrix products, arithmetic and copies ran while one was open for 4% of the time, Pallas kernels for 0%

commit v1 on v0

v1 whole, which is shorter than its diff:
```python
import functools

import jax
import jax.numpy as jnp
from jax import lax
from jax.experimental import pallas as pl
from jax.experimental.pallas import tpu as pltpu
from jax.sharding import PartitionSpec as P

ROPE = 64
VHEAD = 128
EPSILON = 1e-06
MESH = pl.DeviceIdType.MESH
BF16 = jnp.bfloat16
F32 = jnp.float32
LANES = 128


def dot(a, b):
    return jnp.dot(a, b, preferred_element_type=F32)


def dot_nt(a, b, precision=None):
    return lax.dot_general(
        a, b, (((1,), (1,)), ((), ())), preferred_element_type=F32, precision=precision
    )


def near_first(count):
    return sorted(range(1, count), key=lambda d: (min(d, count - d), d))


def kernel(
    sizes,
    width,
    lengths_ref,
    expert_slot_ref,
    queries_ref,
    residual_ref,
    gain_ref,
    router_ref,
    routes_ref,
    cache_hbm,
    value_up_hbm,
    out_proj_hbm,
    gate_up_hbm,
    down_hbm,
    out_ref,
    cache,
    value_up,
    out_proj,
    gate_up,
    down,
    latent,
    heads,
    proj_out,
    proj_in,
    residual,
    extra,
    stream,
    rows,
    wide,
    weights,
    weights_out,
    router_all,
    router_rows,
    part_out,
    part_in,
    tail_out,
    tail_in,
    hidden,
    down_out,
    down_in,
    sum_out,
    sum_in,
    load_sem,
    head_send,
    head_recv,
    head_core_send,
    head_core_recv,
    weight_send,
    weight_recv,
    router_send,
    router_recv,
    proj_send,
    proj_recv,
    row_z_send,
    row_z_recv,
    row_x_send,
    row_x_recv,
    row_core_send,
    row_core_recv,
    part_send,
    part_recv,
    tail_send,
    tail_recv,
    hid_send,
    hid_recv,
    hid_core_send,
    hid_core_recv,
    down_send,
    down_recv,
    sum_send,
    sum_recv,
):
    nx, ny, nz = sizes
    g = lax.axis_index("grp")
    dp = lax.axis_index("dp")
    t = lax.axis_index("tensor")
    y = dp // 2
    c = lax.rem(dp, 2)
    other = 1 - c
    cols = residual_ref.shape[1]
    block = residual_ref.shape[0]
    wide_cols = stream.shape[1]
    seqs, head_count, depth = queries_ref.shape
    latent_dim = value_up.shape[1]
    local_experts = router_ref.shape[0]
    ys, zs = near_first(ny), near_first(nz)
    xs = near_first(nx)

    def at_x(d):
        return lax.rem(g + nx + d, nx)

    def at_y(d):
        return lax.rem(y + ny + d, ny)

    def at_z(d):
        return lax.rem(t + nz + d, nz)

    def to_x(d):
        return (at_x(d), dp, t)

    def to_y(d):
        return (g, at_y(d) * 2 + c, t)

    def to_z(d):
        return (g, dp, at_z(d))

    partner = (g, y * 2 + other, t)
    sent = []

    def send(src, dst, send_sem, recv_sem, device):
        copy = pltpu.make_async_remote_copy(
            src_ref=src,
            dst_ref=dst,
            send_sem=send_sem,
            recv_sem=recv_sem,
            device_id=device,
            device_id_type=MESH,
        )
        copy.start()
        sent.append(copy)

    def arrived(dst, recv_sem):
        pltpu.make_async_remote_copy(
            src_ref=dst,
            dst_ref=dst,
            send_sem=load_sem.at[0],
            recv_sem=recv_sem,
            device_id=partner,
            device_id_type=MESH,
        ).wait_recv()

    barrier = pltpu.get_barrier_semaphore()
    peers = [partner] + [to_y(d) for d in ys] + [to_z(d) for d in zs] + [to_x(d) for d in xs]
    for device in peers:
        pl.semaphore_signal(barrier, inc=1, device_id=device, device_id_type=MESH)

    loads = [
        pltpu.make_async_copy(src, dst, load_sem.at[i])
        for i, (src, dst) in enumerate(
            [
                (cache_hbm, cache),
                (value_up_hbm, value_up),
                (out_proj_hbm, out_proj),
                (gate_up_hbm, gate_up),
            ]
            + [
                (down_hbm.at[e], down.at[:, pl.ds(e * down_hbm.shape[2], down_hbm.shape[2])])
                for e in range(local_experts)
            ]
        )
    ]
    for load in loads:
        load.start()

    score_scale = (VHEAD + ROPE) ** (-0.5)
    loads[0].wait()
    for n in range(seqs):
        scores = dot(queries_ref[n], cache[n]) * score_scale
        positions = lax.broadcasted_iota(jnp.int32, scores.shape, 1)
        scores = jnp.where(positions < lengths_ref[n], scores, -1e30)
        exps = jnp.exp(scores - jnp.max(scores, axis=1, keepdims=True))
        probs = (exps / jnp.sum(exps, axis=1, keepdims=True)).astype(BF16)
        of_seq = dot_nt(probs, cache[n, :latent_dim, :])
        for q in range(latent_dim // LANES):
            latent[q, n * head_count : (n + 1) * head_count, :] = of_seq[
                :, q * LANES : (q + 1) * LANES
            ]
    loads[1].wait()
    half = head_count // 2
    for low in range(half):
        pair = []
        for h in (low, low + half):
            of_head = jnp.concatenate(
                [
                    latent[q, pl.ds(h, seqs, stride=head_count), :]
                    for q in range(latent_dim // LANES)
                ],
                axis=1,
            )
            pair.append(dot(of_head.astype(BF16), value_up[h]))
        heads[y, c, :, low * VHEAD : (low + 1) * VHEAD] = jnp.concatenate(pair, axis=0).astype(
            BF16
        )

    pl.semaphore_wait(barrier, len(peers))

    mine = heads.at[y, c]
    for d in ys:
        send(mine, mine, head_send.at[d], head_recv.at[d], to_y(d))
    send(mine, mine, head_core_send.at[0], head_core_recv.at[0], partner)

    gain_row = gain_ref[...].astype(F32)
    router_all[c, g] = jnp.zeros(router_all.shape[2:], F32)
    router_all[c, g, :local_experts, :cols] = router_ref[...].astype(F32) * gain_row
    for d in xs:
        send(
            router_all.at[c, g], router_all.at[c, g], router_send.at[d], router_recv.at[d], to_x(d)
        )
    identity = (
        lax.broadcasted_iota(jnp.int32, (cols, cols), 0)
        == lax.broadcasted_iota(jnp.int32, (cols, cols), 1)
    ).astype(F32)
    gain_column = dot_nt(
        identity.astype(BF16), jnp.broadcast_to(gain_row, (LANES, cols)).astype(BF16)
    )
    loads[3].wait()
    for dst, first in ((weights_out, other * 2), (weights.at[c], c * 2)):
        dst[cols:, :] = jnp.zeros((wide_cols - cols, dst.shape[1]), BF16)
        for j in range(2):
            wide[...] = gate_up[first + j].astype(F32)
            for i in range(2):
                part = wide[pl.ds(i, cols, stride=2), :] * gain_column
                start = (2 * j + i) * LANES
                dst[:cols, start : start + LANES] = part.astype(BF16)
        if dst is weights_out:
            send(weights_out, weights.at[c], weight_send, weight_recv, partner)

    lane = lax.broadcasted_iota(jnp.int32, (block, LANES), 1)
    routes = routes_ref[...]
    slot_of = jnp.zeros(routes.shape, jnp.int32)
    for e in range(expert_slot_ref.shape[0]):
        slot_of = jnp.where(routes == e, expert_slot_ref[e], slot_of)
    used = cols - (wide_cols - LANES)
    slots = expert_slot_ref.shape[0]
    by_slot = jnp.zeros((slots, block), F32)
    slot_at = lax.broadcasted_iota(jnp.int32, (slots, block), 0)
    for k in range(routes.shape[0]):
        by_slot = by_slot + (slot_at == slot_of[k : k + 1, :]).astype(F32)
    same = lax.broadcasted_iota(jnp.int32, (block, block), 0) == lax.broadcasted_iota(
        jnp.int32, (block, block), 1
    )
    by_token = dot_nt(same.astype(F32), by_slot)
    place = lax.broadcasted_iota(jnp.int32, (slots, LANES), 1) - used
    place = (place == lax.broadcasted_iota(jnp.int32, (slots, LANES), 0)).astype(F32)
    extra[...] = dot(by_token, place)
    residual[:, wide_cols - LANES :] = jnp.zeros((block, LANES), F32)
    residual[:, :cols] = residual_ref[...].astype(F32)
    proj_out[:, :, wide_cols - LANES :] = jnp.zeros((nz, block, LANES), BF16)

    for d in ys:
        came = heads.at[at_y(-d), c]
        arrived(came, head_recv.at[d])
        send(came, came, head_core_send.at[d], head_core_recv.at[d], partner)
    loads[2].wait()
    for d in [0] + ys:
        arrived(heads.at[at_y(-d), other], head_core_recv.at[d])

    gathered = heads[...].reshape(ny * 2 * 2 * seqs, half * VHEAD)
    low_part = dot_nt(gathered, out_proj[:, : half * VHEAD]).reshape(ny * 2, 2, seqs, cols)
    high_part = dot_nt(gathered, out_proj[:, half * VHEAD :]).reshape(ny * 2, 2, seqs, cols)
    attn = (low_part[:, 0] + high_part[:, 1]).reshape(nz, block, cols)
    proj_out[:, :, :cols] = attn.astype(BF16)
    for d in zs:
        send(proj_out.at[at_z(d)], proj_in.at[t], proj_send.at[d], proj_recv.at[d], to_z(d))

    for d in xs:
        arrived(router_all.at[c, at_x(-d)], router_recv.at[d])
    send(router_all.at[c], router_all.at[c], router_send.at[0], router_recv.at[0], partner)
    arrived(weights.at[other], weight_recv)
    arrived(router_all.at[other], router_recv.at[0])
    pad = router_all.shape[2]
    slot_row = lax.broadcasted_iota(jnp.int32, (slots, nx * pad), 0)
    select = (
        lax.broadcasted_iota(jnp.int32, (slots, nx * pad), 1)
        == (slot_row // local_experts) * pad + lax.rem(slot_row, local_experts)
    ).astype(F32).astype(BF16)
    column = lax.broadcasted_iota(jnp.int32, (slots, wide_cols), 1)
    squares_at = (column == cols + slots) | (column == cols + slots + 1)
    for core in range(2):
        packed = router_all[core].reshape(nx * pad, wide_cols).astype(BF16)
        router_rows[core, :slots] = dot(select, packed).astype(BF16)
        router_rows[core, slots:] = squares_at.astype(F32).astype(BF16)

    total = residual[...] + proj_out[t].astype(F32)
    for d in zs:
        arrived(proj_in.at[at_z(-d)], proj_recv.at[d])
        total = total + proj_in[at_z(-d)].astype(F32)
    total = total.astype(BF16).astype(F32)
    stream[...] = total
    squares = jnp.sum(total * total, axis=1, keepdims=True)
    upper = squares.astype(BF16).astype(F32)
    marks = extra[...]
    marks = jnp.where(lane == used + slots, upper, marks)
    marks = jnp.where(lane == used + slots + 1, squares - upper, marks)
    rows[c, g, t, :, : wide_cols - LANES] = total[:, : wide_cols - LANES].astype(BF16)
    rows[c, g, t, :, wide_cols - LANES :] = (total[:, wide_cols - LANES :] + marks).astype(BF16)

    mine = rows.at[c, g, t]
    for d in zs:
        send(mine, mine, row_z_send.at[d], row_z_recv.at[d], to_z(d))
    for a in xs:
        send(mine, mine, row_x_send.at[a, 0], row_x_recv.at[a], to_x(a))
    for d in zs:
        came = rows.at[c, g, at_z(-d)]
        arrived(came, row_z_recv.at[d])
        for a in xs:
            send(came, came, row_x_send.at[a, d], row_x_recv.at[a], to_x(a))
    for a in [0] + xs:
        came = rows.at[c, at_x(-a)]
        if a:
            arrived(came, row_x_recv.at[a])
        send(came, came, row_core_send.at[a], row_core_recv.at[a], partner)
        arrived(rows.at[other, at_x(-a)], row_core_recv.at[a])
        of = at_x(-a)
        part = dot(rows[0, of].reshape(nz * block, wide_cols), weights[0])
        part = part + dot(rows[1, of].reshape(nz * block, wide_cols), weights[1])
        part_out[of] = part.astype(BF16).reshape(nz, block, part.shape[1])
        for d in ys:
            send(
                part_out.at[of, at_y(d)],
                part_in.at[y, of],
                part_send.at[d, a],
                part_recv.at[d],
                to_y(d),
            )

    chunk = nx * block
    tail = jnp.zeros((2 * slots, ny * chunk), F32)
    for core in range(2):
        by_owner = jnp.concatenate([rows[core, :, k].reshape(chunk, wide_cols) for k in range(nz)])
        tail = tail + dot_nt(router_rows[core], by_owner)
    lane_of = lax.broadcasted_iota(jnp.int32, (slots, LANES), 1)
    for j in range(ny * chunk // LANES):
        logits = tail[:slots, j * LANES : (j + 1) * LANES]
        sums = tail[slots:, j * LANES : (j + 1) * LANES]
        even = jnp.where(lane_of < chunk, logits, pltpu.roll(sums, chunk, 1))
        odd = jnp.where(lane_of < chunk, pltpu.roll(logits, chunk, 1), sums)
        tail_out[2 * j] = even.astype(BF16)
        tail_out[2 * j + 1] = odd.astype(BF16)
    for d in ys:
        send(tail_out.at[at_y(d)], tail_in.at[y], tail_send.at[d], tail_recv.at[d], to_y(d))

    total = part_out[:, y].astype(F32)
    tail = tail_out[y].astype(F32)
    for d in ys:
        arrived(part_in.at[at_y(-d)], part_recv.at[d])
        total = total + part_in[at_y(-d)].astype(F32)
    for d in ys:
        arrived(tail_in.at[at_y(-d)], tail_recv.at[d])
        tail = tail + tail_in[at_y(-d)].astype(F32)
    total = total.reshape(chunk, total.shape[2])
    down_at = lax.broadcasted_iota(jnp.int32, (chunk, LANES), 0)
    across = lax.broadcasted_iota(jnp.int32, (chunk, LANES), 1)
    logits = dot_nt((across == down_at).astype(F32), tail, lax.Precision.HIGHEST)
    sums = dot_nt((across == down_at + chunk).astype(F32), tail, lax.Precision.HIGHEST)
    inv_rms = lax.rsqrt(sums / width + EPSILON)
    marks = rows[c, :, y, :, wide_cols - LANES :].reshape(chunk, LANES).astype(F32)
    marks = pltpu.roll(marks, LANES - used, 1)[:, :slots]
    scores = jax.nn.sigmoid(logits * inv_rms) * marks
    shares = scores / jnp.sum(scores, axis=1, keepdims=True)
    slot_at = lax.broadcasted_iota(jnp.int32, (chunk, slots), 1)
    inv_rms = inv_rms[:, :1]
    for j in range(2):
        chosen = slot_at == g * local_experts + c * 2 + j
        share = jnp.sum(jnp.where(chosen, shares, 0.0), axis=1, keepdims=True)
        gate = total[:, 2 * j * LANES : (2 * j + 1) * LANES] * inv_rms
        up = total[:, (2 * j + 1) * LANES : (2 * j + 2) * LANES] * inv_rms
        value = jax.nn.silu(gate) * up * share
        hidden[c, y, :, j * LANES : (j + 1) * LANES] = value.astype(BF16)

    mine = hidden.at[c, y]
    for d in ys:
        send(mine, mine, hid_send.at[d], hid_recv.at[d], to_y(d))
    send(mine, mine, hid_core_send.at[0], hid_core_recv.at[0], partner)
    for load in loads[4:]:
        load.wait()
    down_out[:, :, :, wide_cols - LANES :] = jnp.zeros(down_out.shape[:3] + (LANES,), BF16)
    split = down.shape[1] // 2
    for d in [0] + ys:
        of = at_y(-d)
        if d:
            came = hidden.at[c, of]
            arrived(came, hid_recv.at[d])
            send(came, came, hid_core_send.at[d], hid_core_recv.at[d], partner)
        arrived(hidden.at[other, of], hid_core_recv.at[d])
        part = dot_nt(hidden[0, of], down[:, :split]) + dot_nt(hidden[1, of], down[:, split:])
        down_out[of, :, :, :cols] = part.astype(BF16).reshape(nx, block, cols)
        for a in xs:
            send(
                down_out.at[of, at_x(a)],
                down_in.at[a, of],
                down_send.at[a, d],
                down_recv.at[a, of],
                to_x(a),
            )

    for d in sorted(range(nz), key=lambda d: -min(d, nz - d)):
        of = at_z(d)
        total = down_out[of, g].astype(F32)
        for a in xs:
            arrived(down_in.at[a, of], down_recv.at[a, of])
            total = total + down_in[a, of].astype(F32)
        if d:
            sum_out[d] = total.astype(BF16)
            send(sum_out.at[d], sum_in.at[d], sum_send.at[d], sum_recv.at[d], to_z(d))
    total = total + stream[...]
    for d in zs:
        arrived(sum_in.at[d], sum_recv.at[d])
        total = total + sum_in[d].astype(F32)
    out_ref[...] = total[:, :cols].astype(BF16)

    for copy in sent:
        copy.wait_send()


def on_device(sizes, width, *arrays):
    (
        queries,
        latent_cache,
        lengths,
        value_up,
        out_proj,
        residual_in,
        norm_gain,
        router,
        gate_up,
        down_proj,
        routes,
        expert_slot,
    ) = arrays
    nx, ny, nz = sizes
    seqs, head_count, depth = queries.shape
    block, cols = residual_in.shape
    experts, _, _, units = gate_up.shape
    gate_up = gate_up.reshape(experts, cols * 2, units)
    down_proj = jnp.swapaxes(down_proj, 1, 2)
    latent_cache = jnp.swapaxes(latent_cache, 1, 2)
    out_proj = out_proj.T
    routes = routes.T
    gain = norm_gain.reshape(1, cols)
    wide_cols = -(-cols // LANES) * LANES
    latent_dim = value_up.shape[1]
    slots = expert_slot.shape[0]
    chunk = nx * block
    vmem = pl.BlockSpec(memory_space=pltpu.VMEM)
    smem = pl.BlockSpec(memory_space=pltpu.SMEM)
    anywhere = pl.BlockSpec(memory_space=pltpu.HBM)
    sem = pltpu.SemaphoreType.DMA
    scratch = [
        pltpu.VMEM(latent_cache.shape, BF16),
        pltpu.VMEM(value_up.shape, BF16),
        pltpu.VMEM(out_proj.shape, BF16),
        pltpu.VMEM(gate_up.shape, BF16),
        pltpu.VMEM((cols, experts * units), BF16),
        pltpu.VMEM((latent_dim // LANES, seqs * head_count, LANES), F32),
        pltpu.VMEM((ny, 2, 2 * seqs, head_count // 2 * VHEAD), BF16),
        pltpu.VMEM((nz, block, wide_cols), BF16),
        pltpu.VMEM((nz, block, wide_cols), BF16),
        pltpu.VMEM((block, wide_cols), F32),
        pltpu.VMEM((block, LANES), F32),
        pltpu.VMEM((block, wide_cols), F32),
        pltpu.VMEM((2, nx, nz, block, wide_cols), BF16),
        pltpu.VMEM((cols * 2, units), F32),
        pltpu.VMEM((2, wide_cols, 4 * units), BF16),
        pltpu.VMEM((wide_cols, 4 * units), BF16),
        pltpu.VMEM((2, nx, 8, wide_cols), F32),
        pltpu.VMEM((2, 2 * slots, wide_cols), BF16),
        pltpu.VMEM((nx, nz, block, 4 * units), BF16),
        pltpu.VMEM((ny, nx, block, 4 * units), BF16),
        pltpu.VMEM((ny, slots, LANES), BF16),
        pltpu.VMEM((ny, slots, LANES), BF16),
        pltpu.VMEM((2, ny, chunk, 2 * units), BF16),
        pltpu.VMEM((ny, nx, block, wide_cols), BF16),
        pltpu.VMEM((nx, ny, block, wide_cols), BF16),
        pltpu.VMEM((nz, block, wide_cols), BF16),
        pltpu.VMEM((nz, block, wide_cols), BF16),
        sem((4 + experts,)),
        sem((ny,)),
        sem((ny,)),
        sem((ny,)),
        sem((ny,)),
        sem,
        sem,
        sem((nx,)),
        sem((nx,)),
        sem((nz,)),
        sem((nz,)),
        sem((nz,)),
        sem((nz,)),
        sem((nx, nz)),
        sem((nx,)),
        sem((nx,)),
        sem((nx,)),
        sem((ny, nx)),
        sem((ny,)),
        sem((ny,)),
        sem((ny,)),
        sem((ny,)),
        sem((ny,)),
        sem((ny,)),
        sem((ny,)),
        sem((nx, ny)),
        sem((nx, ny)),
        sem((nz,)),
        sem((nz,)),
    ]
    return pl.pallas_call(
        functools.partial(kernel, sizes, width),
        out_shape=jax.ShapeDtypeStruct((block, cols), BF16),
        in_specs=[smem, smem, vmem, vmem, vmem, vmem, vmem] + [anywhere] * 5,
        out_specs=vmem,
        scratch_shapes=scratch,
        name="decode_layer",
        compiler_params=pltpu.CompilerParams(
            collective_id=0, has_side_effects=True, vmem_limit_bytes=60 * 2**20
        ),
    )(
        lengths,
        expert_slot,
        queries,
        residual_in,
        gain,
        router,
        routes,
        latent_cache,
        value_up,
        out_proj,
        gate_up,
        down_proj,
    )


def solution(mesh):
    in_specs = (
        P(("grp", "dp"), "tensor", None),
        P(("grp", "dp"), None, None),
        P(("grp", "dp")),
        P("tensor", None, None),
        P("tensor", "dp"),
        P(("grp", "tensor"), "dp"),
        P("dp"),
        P("grp", "dp"),
        P("grp", "dp", None, "tensor"),
        P("grp", "tensor", "dp"),
        P(("grp", "tensor"), None),
        P(),
    )
    out_specs = P(("grp", "tensor"), "dp")
    sizes = (mesh.shape["grp"], mesh.shape["dp"] // 2, mesh.shape["tensor"])

    def whole(*arrays):
        width = arrays[5].shape[1]
        return jax.shard_map(
            functools.partial(on_device, sizes, width),
            mesh=mesh,
            in_specs=in_specs,
            out_specs=out_specs,
            check_vma=False,
        )(*arrays)

    return whole
```

time: 337 us -> 80.2 us (0.24)
  waiting for transfers between devices: 195 us -> 0 us
  Pallas kernels: 0 us -> 77.4 us
  blocking collectives: 75 us -> 0 us
  starting transfers between devices: 22.4 us -> 0 us
  between operations: 13.6 us -> 0.01 us
  matrix products: 13.1 us -> 0 us
  other arithmetic: 6.75 us -> 0 us
  local copies, waits for them, and re-layouts: 8.03 us -> 2.58 us
    all_to_all x3 -> x0, waiting for transfers between devices: 99.8 us -> none  [the longest x1 70.7 us: on_device(): lax.all_to_all(flat_term, ('grp', 'tensor'), split_axis=0, concat_axis=0,...]
    pallas_call x0 -> x1, Pallas kernels: none -> 77.4 us  [on_device(): pl.pallas_call(functools.partial(kernel, sizes, width), out_shape=jax.Sha...]
    psum x1 -> x0, waiting for transfers between devices: 62.4 us -> none  [on_device(): lax.psum((gate_up_sum, router_logit, squares), 'dp')]
    psum x1 -> x0, blocking collectives: 53.5 us -> none  [on_device(): lax.psum((gate_up_sum, router_logit, squares), 'dp')]
    reduce_scatter x1 -> x0, waiting for transfers between devices: 33.1 us -> none  [on_device(): lax.psum_scatter(jnp.dot(gathered, out_proj, preferred_element_type=jnp.f...]
    all_to_all x3 -> x0, starting transfers between devices: 22.4 us -> none  [the longest x1 10 us: on_device(): lax.all_to_all(flat_term, ('grp', 'tensor'), split_axis=0, concat_axis=0,...]
    all_gather x1 -> x0, blocking collectives: 21.6 us -> none  [on_device(): gathered = lax.all_gather(head_out, 'dp', axis=0, tiled=True)]
    dot_general x10 -> x0, matrix products: 13.1 us -> none  [the longest x1 2.48 us: on_device(): jnp.einsum('secd,ed->sec', scaled, router, preferred_element_type=jnp.flo...]
  transfers between devices with their start and end apart: 5 -> 0, of which waited for: 4 -> 0; matrix products, arithmetic and copies ran while one was open for 4% -> 0% of each run, Pallas kernels for 0% -> 0%
where the time goes in v1:
time: 80.2 us; the launch traced here: 80 us
  Pallas kernels  77.4 us (97%)
  local copies, waits for them, and re-layouts  2.58 us (3%)
    pallas_call x1, Pallas kernels, on_device(): pl.pallas_call(functools.partial(kernel, sizes, width), out_shape=jax.Sha...  77.4 us

profile of v1, /device:TPU:1, one launch (start us, length us, event | category | flops | bytes accessed | tf_op | source)
XLA Modules:
  0.0 80.0 jit_solution(17772356429198316802)
XLA Ops:
  0.0 1.3 %reshape.6.gain_ref = bf16[1,448]{1,0:T(2,128)(2,1)} reshape(bf16[448]{0:T(512)(128)(2,1)} %param.18) | data formatting | bytes 1792 | tf_op jit(solution)/shard_map/reshape | solution.py:463
  1.3 77.4 %decode_layer.1 = bf16[16,448]{1,0:T(8,128)(2,1)} custom-call(s32[8]{0:T(128)} %lengths_ref.1, s32[16]{0:T(128)} %expert_slot_ref.1, bf16[8,8,576]{2,1,0:T(8,128)(2,1)} %queries_ref.1, bf16[16,448]{1,0:T(8,128)(2,1)} %residual_ref.1, bf16[1,448]{1,0:T(2,128)(2,1)} %reshape.6.gain_ref, bf16[4,448]{1,0:T(4,128)(2,1)} %router_ref.1, s32[8,16]{1,0:T(8,128)} %bitcast.9, ...), custom_call_target="tpu_custom_call" | custom-call | tf_op jit(solution)/shard_map/decode_layer/pallas_call | solution.py:530
  78.7 1.3 %copy.14 = bf16[16,448]{1,0:T(8,128)(2,1)} copy(bf16[16,448]{1,0:T(8,128)(2,1)} %decode_layer.1) | data formatting | bytes 28672

commit v2 on v1

--- a/solution.py
+++ b/solution.py
@@ -33,6 +33,19 @@
 def kernel(
     sizes,
     width,
+    lengths_hbm,
+    expert_slot_hbm,
+    queries_hbm,
+    residual_hbm,
+    gain_hbm,
+    router_hbm,
+    routes_hbm,
+    cache_hbm,
+    value_up_hbm,
+    out_proj_hbm,
+    gate_up_hbm,
+    down_hbm,
+    out_ref,
     lengths_ref,
     expert_slot_ref,
     queries_ref,
@@ -40,12 +53,6 @@
     gain_ref,
     router_ref,
     routes_ref,
-    cache_hbm,
-    value_up_hbm,
-    out_proj_hbm,
-    gate_up_hbm,
-    down_hbm,
-    out_ref,
     cache,
     value_up,
     out_proj,
@@ -74,6 +81,7 @@
     sum_out,
     sum_in,
     load_sem,
+    small_sem,
     head_send,
     head_recv,
     head_core_send,
@@ -117,10 +125,11 @@
     latent_dim = value_up.shape[1]
     local_experts = router_ref.shape[0]
     ys, zs = near_first(ny), near_first(nz)
-    xs = near_first(nx)
-
-    def at_x(d):
-        return lax.rem(g + nx + d, nx)
+    xs = [1, 3, 2]
+    far_ys, far_zs = ys[::-1], zs[::-1]
+
+    def at_x(code):
+        return [g, g + 1 - 2 * lax.rem(g, 2), lax.rem(g + 2, nx), nx - 1 - g][code]
 
     def at_y(d):
         return lax.rem(y + ny + d, ny)
@@ -166,6 +175,21 @@
     peers = [partner] + [to_y(d) for d in ys] + [to_z(d) for d in zs] + [to_x(d) for d in xs]
     for device in peers:
         pl.semaphore_signal(barrier, inc=1, device_id=device, device_id_type=MESH)
+
+    small = [
+        pltpu.make_async_copy(src, dst, small_sem.at[i])
+        for i, (src, dst) in enumerate(
+            [
+                (lengths_hbm, lengths_ref),
+                (queries_hbm, queries_ref),
+                (expert_slot_hbm, expert_slot_ref),
+                (gain_hbm, gain_ref),
+                (router_hbm, router_ref),
+                (routes_hbm, routes_ref),
+                (residual_hbm, residual_ref),
+            ]
+        )
+    ]
 
     loads = [
         pltpu.make_async_copy(src, dst, load_sem.at[i])
@@ -182,10 +206,12 @@
             ]
         )
     ]
-    for load in loads:
+    for load in small[:2] + loads[:1] + small[2:] + loads[1:]:
         load.start()
 
     score_scale = (VHEAD + ROPE) ** (-0.5)
+    for load in small[:2]:
+        load.wait()
     loads[0].wait()
     for n in range(seqs):
         scores = dot(queries_ref[n], cache[n]) * score_scale
@@ -218,11 +244,13 @@
     pl.semaphore_wait(barrier, len(peers))
 
     mine = heads.at[y, c]
-    for d in ys:
+    for d in far_ys:
         send(mine, mine, head_send.at[d], head_recv.at[d], to_y(d))
     send(mine, mine, head_core_send.at[0], head_core_recv.at[0], partner)
 
-    gain_row = gain_ref[...].astype(F32)
+    for load in small[2:]:
+        load.wait()
+    gain_row = gain_ref[...].astype(F32)[None, :]
     router_all[c, g] = jnp.zeros(router_all.shape[2:], F32)
     router_all[c, g, :local_experts, :cols] = router_ref[...].astype(F32) * gain_row
     for d in xs:
@@ -283,11 +311,11 @@
     high_part = dot_nt(gathered, out_proj[:, half * VHEAD :]).reshape(ny * 2, 2, seqs, cols)
     attn = (low_part[:, 0] + high_part[:, 1]).reshape(nz, block, cols)
     proj_out[:, :, :cols] = attn.astype(BF16)
-    for d in zs:
+    for d in far_zs:
         send(proj_out.at[at_z(d)], proj_in.at[t], proj_send.at[d], proj_recv.at[d], to_z(d))
 
     for d in xs:
-        arrived(router_all.at[c, at_x(-d)], router_recv.at[d])
+        arrived(router_all.at[c, at_x(d)], router_recv.at[d])
     send(router_all.at[c], router_all.at[c], router_send.at[0], router_recv.at[0], partner)
     arrived(weights.at[other], weight_recv)
     arrived(router_all.at[other], router_recv.at[0])
@@ -319,118 +347,193 @@
     rows[c, g, t, :, wide_cols - LANES :] = (total[:, wide_cols - LANES :] + marks).astype(BF16)
 
     mine = rows.at[c, g, t]
-    for d in zs:
+    for d in far_zs:
         send(mine, mine, row_z_send.at[d], row_z_recv.at[d], to_z(d))
-    for a in xs:
+    for a in (2, 1, 3):
         send(mine, mine, row_x_send.at[a, 0], row_x_recv.at[a], to_x(a))
     for d in zs:
         came = rows.at[c, g, at_z(-d)]
         arrived(came, row_z_recv.at[d])
-        for a in xs:
+        for a in (2, 1, 3):
             send(came, came, row_x_send.at[a, d], row_x_recv.at[a], to_x(a))
-    for a in [0] + xs:
-        came = rows.at[c, at_x(-a)]
+    def pass_rows(a):
+        came = rows.at[c, at_x(a)]
         if a:
             arrived(came, row_x_recv.at[a])
         send(came, came, row_core_send.at[a], row_core_recv.at[a], partner)
-        arrived(rows.at[other, at_x(-a)], row_core_recv.at[a])
-        of = at_x(-a)
-        part = dot(rows[0, of].reshape(nz * block, wide_cols), weights[0])
-        part = part + dot(rows[1, of].reshape(nz * block, wide_cols), weights[1])
+
+    def multiply_rows(a):
+        of = at_x(a)
+        part = dot(rows[c, of].reshape(nz * block, wide_cols), weights[c])
+        arrived(rows.at[other, of], row_core_recv.at[a])
+        part = part + dot(rows[other, of].reshape(nz * block, wide_cols), weights[other])
         part_out[of] = part.astype(BF16).reshape(nz, block, part.shape[1])
-        for d in ys:
+        of_half, place = [(0, 0), (1, 0), (0, 1), (1, 1)][a]
+        for d in far_ys:
             send(
                 part_out.at[of, at_y(d)],
-                part_in.at[y, of],
+                part_in.at[of_half, y, place],
                 part_send.at[d, a],
-                part_recv.at[d],
+                part_recv.at[of_half, d],
                 to_y(d),
             )
 
-    chunk = nx * block
-    tail = jnp.zeros((2 * slots, ny * chunk), F32)
-    for core in range(2):
-        by_owner = jnp.concatenate([rows[core, :, k].reshape(chunk, wide_cols) for k in range(nz)])
-        tail = tail + dot_nt(router_rows[core], by_owner)
-    lane_of = lax.broadcasted_iota(jnp.int32, (slots, LANES), 1)
-    for j in range(ny * chunk // LANES):
-        logits = tail[:slots, j * LANES : (j + 1) * LANES]
-        sums = tail[slots:, j * LANES : (j + 1) * LANES]
-        even = jnp.where(lane_of < chunk, logits, pltpu.roll(sums, chunk, 1))
-        odd = jnp.where(lane_of < chunk, pltpu.roll(logits, chunk, 1), sums)
-        tail_out[2 * j] = even.astype(BF16)
-        tail_out[2 * j + 1] = odd.astype(BF16)
-    for d in ys:
-        send(tail_out.at[at_y(d)], tail_in.at[y], tail_send.at[d], tail_recv.at[d], to_y(d))
-
-    total = part_out[:, y].astype(F32)
-    tail = tail_out[y].astype(F32)
-    for d in ys:
-        arrived(part_in.at[at_y(-d)], part_recv.at[d])
-        total = total + part_in[at_y(-d)].astype(F32)
-    for d in ys:
-        arrived(tail_in.at[at_y(-d)], tail_recv.at[d])
-        tail = tail + tail_in[at_y(-d)].astype(F32)
-    total = total.reshape(chunk, total.shape[2])
+    chunk = 2 * block
+    halves = ((0, 2), (1, 3))
+    per_tile = LANES // chunk
+
+    def send_tail(h):
+        missing = max(LANES - nz * chunk, 0)
+        tail = jnp.zeros((2 * slots, nz * chunk + missing), F32)
+        for core in range(2):
+            by_owner = jnp.concatenate(
+                [
+                    rows[core, at_x(code)].reshape(nz, 1, block, wide_cols)
+                    for code in halves[h]
+                ],
+                axis=1,
+            ).reshape(nz * chunk, wide_cols)
+            if missing:
+                by_owner = jnp.concatenate([by_owner, jnp.zeros((missing, wide_cols), BF16)])
+            tail = tail + dot_nt(router_rows[core], by_owner)
+        lane_of = lax.broadcasted_iota(jnp.int32, (slots, LANES), 1)
+        for q in range(ny):
+            tile = slice(q // per_tile * LANES, (q // per_tile + 1) * LANES)
+            turn = LANES - q % per_tile * chunk
+            logits = pltpu.roll(tail[:slots, tile], turn % LANES, 1)
+            sums = pltpu.roll(tail[slots:, tile], (turn + chunk) % LANES, 1)
+            tail_out[h, q] = jnp.where(lane_of < chunk, logits, sums).astype(BF16)
+        for d in far_ys:
+            send(
+                tail_out.at[h, at_y(d)],
+                tail_in.at[h, y],
+                tail_send.at[h, d],
+                tail_recv.at[h, d],
+                to_y(d),
+            )
+
+    pass_rows(0)
+    multiply_rows(0)
+    pass_rows(2)
+    pass_rows(1)
+    multiply_rows(2)
+    send_tail(0)
+    pass_rows(3)
+    multiply_rows(1)
+    multiply_rows(3)
+    send_tail(1)
+
     down_at = lax.broadcasted_iota(jnp.int32, (chunk, LANES), 0)
     across = lax.broadcasted_iota(jnp.int32, (chunk, LANES), 1)
-    logits = dot_nt((across == down_at).astype(F32), tail, lax.Precision.HIGHEST)
-    sums = dot_nt((across == down_at + chunk).astype(F32), tail, lax.Precision.HIGHEST)
-    inv_rms = lax.rsqrt(sums / width + EPSILON)
-    marks = rows[c, :, y, :, wide_cols - LANES :].reshape(chunk, LANES).astype(F32)
-    marks = pltpu.roll(marks, LANES - used, 1)[:, :slots]
-    scores = jax.nn.sigmoid(logits * inv_rms) * marks
-    shares = scores / jnp.sum(scores, axis=1, keepdims=True)
     slot_at = lax.broadcasted_iota(jnp.int32, (chunk, slots), 1)
-    inv_rms = inv_rms[:, :1]
-    for j in range(2):
-        chosen = slot_at == g * local_experts + c * 2 + j
-        share = jnp.sum(jnp.where(chosen, shares, 0.0), axis=1, keepdims=True)
-        gate = total[:, 2 * j * LANES : (2 * j + 1) * LANES] * inv_rms
-        up = total[:, (2 * j + 1) * LANES : (2 * j + 2) * LANES] * inv_rms
-        value = jax.nn.silu(gate) * up * share
-        hidden[c, y, :, j * LANES : (j + 1) * LANES] = value.astype(BF16)
-
-    mine = hidden.at[c, y]
-    for d in ys:
-        send(mine, mine, hid_send.at[d], hid_recv.at[d], to_y(d))
-    send(mine, mine, hid_core_send.at[0], hid_core_recv.at[0], partner)
+
+    def find_hidden(h):
+        tail = tail_out[h, y].astype(F32)
+        total = jnp.concatenate([part_out[at_x(code), y] for code in halves[h]]).astype(F32)
+        for d in ys:
+            of = at_y(-d)
+            arrived(tail_in.at[h, of], tail_recv.at[h, d])
+            tail = tail + tail_in[h, of].astype(F32)
+        for d in ys:
+            of = at_y(-d)
+            arrived(part_in.at[h, of], part_recv.at[h, d])
+            total = total + part_in[h, of].reshape(total.shape).astype(F32)
+        logits = dot_nt((across == down_at).astype(F32), tail, lax.Precision.HIGHEST)
+        sums = dot_nt((across == down_at + chunk).astype(F32), tail, lax.Precision.HIGHEST)
+        inv_rms = lax.rsqrt(sums / width + EPSILON)
+        marks = jnp.concatenate(
+            [rows[c, at_x(code), y, :, wide_cols - LANES :] for code in halves[h]]
+        ).astype(F32)
+        marks = pltpu.roll(marks, LANES - used, 1)[:, :slots]
+        scores = jax.nn.sigmoid(logits * inv_rms) * marks
+        shares = scores / jnp.sum(scores, axis=1, keepdims=True)
+        inv_rms = inv_rms[:, :1]
+        for j in range(2):
+            chosen = slot_at == g * local_experts + c * 2 + j
+            share = jnp.sum(jnp.where(chosen, shares, 0.0), axis=1, keepdims=True)
+            gate = total[:, 2 * j * LANES : (2 * j + 1) * LANES] * inv_rms
+            up = total[:, (2 * j + 1) * LANES : (2 * j + 2) * LANES] * inv_rms
+            value = jax.nn.silu(gate) * up * share
+            hidden[h, c, y, :, j * LANES : (j + 1) * LANES] = value.astype(BF16)
+        mine = hidden.at[h, c, y]
+        for d in ys:
+            send(mine, mine, hid_send.at[h, d], hid_recv.at[h, d], to_y(d))
+        send(mine, mine, hid_core_send.at[h, 0], hid_core_recv.at[h, 0], partner)
+
+    down_out[:, :, :, :, wide_cols - LANES :] = jnp.zeros(down_out.shape[:4] + (LANES,), BF16)
+    find_hidden(0)
+    find_hidden(1)
     for load in loads[4:]:
         load.wait()
-    down_out[:, :, :, wide_cols - LANES :] = jnp.zeros(down_out.shape[:3] + (LANES,), BF16)
     split = down.shape[1] // 2
-    for d in [0] + ys:
+
+    def pass_hidden(h, d):
+        if d:
+            came = hidden.at[h, c, at_y(-d)]
+            arrived(came, hid_recv.at[h, d])
+            send(came, came, hid_core_send.at[h, d], hid_core_recv.at[h, d], partner)
+
+    def multiply_hidden(h, d):
         of = at_y(-d)
-        if d:
-            came = hidden.at[c, of]
-            arrived(came, hid_recv.at[d])
-            send(came, came, hid_core_send.at[d], hid_core_recv.at[d], partner)
-        arrived(hidden.at[other, of], hid_core_recv.at[d])
-        part = dot_nt(hidden[0, of], down[:, :split]) + dot_nt(hidden[1, of], down[:, split:])
-        down_out[of, :, :, :cols] = part.astype(BF16).reshape(nx, block, cols)
-        for a in xs:
-            send(
-                down_out.at[of, at_x(a)],
-                down_in.at[a, of],
-                down_send.at[a, d],
-                down_recv.at[a, of],
-                to_x(a),
-            )
-
-    for d in sorted(range(nz), key=lambda d: -min(d, nz - d)):
-        of = at_z(d)
-        total = down_out[of, g].astype(F32)
-        for a in xs:
-            arrived(down_in.at[a, of], down_recv.at[a, of])
+        arrived(hidden.at[h, other, of], hid_core_recv.at[h, d])
+        part = dot_nt(hidden[h, 0, of], down[:, :split])
+        part = part + dot_nt(hidden[h, 1, of], down[:, split:])
+        down_out[h, of, :, :, :cols] = part.astype(BF16).reshape(2, block, cols)
+        for place, code in enumerate(halves[h]):
+            if code:
+                send(
+                    down_out.at[h, of, place],
+                    down_in.at[code, of],
+                    down_send.at[code, d],
+                    down_recv.at[code, d],
+                    to_x(code),
+                )
+
+    def to_owner(d):
+        return pltpu.make_async_remote_copy(
+            src_ref=sum_out.at[at_y(-d)],
+            dst_ref=sum_in.at[t],
+            send_sem=sum_send.at[d],
+            recv_sem=sum_recv.at[t],
+            device_id=(g, dp, at_y(-d)),
+            device_id_type=MESH,
+        )
+
+    def add_groups(d):
+        of = at_y(-d)
+        total = down_out[0, of, 0].astype(F32)
+        for a in (2, 1, 3):
+            arrived(down_in.at[a, of], down_recv.at[a, d])
             total = total + down_in[a, of].astype(F32)
-        if d:
-            sum_out[d] = total.astype(BF16)
-            send(sum_out.at[d], sum_in.at[d], sum_send.at[d], sum_recv.at[d], to_z(d))
-    total = total + stream[...]
+        sum_out[of] = total.astype(BF16)
+
+        @pl.when(of != t)
+        def _():
+            to_owner(d).start()
+
+    order = [0] + ys
+    steps = [(h, d) for h in range(2) for d in order]
+    pass_hidden(*steps[0])
+    for i, (h, d) in enumerate(steps):
+        if i + 1 < len(steps):
+            pass_hidden(*steps[i + 1])
+        multiply_hidden(h, d)
+        if i - ny >= 2:
+            add_groups(order[i - ny - 2])
+    for d in order[max(ny - 2, 0) :]:
+        add_groups(d)
+    total = stream[...] + sum_out[t].astype(F32)
     for d in zs:
-        arrived(sum_in.at[d], sum_recv.at[d])
-        total = total + sum_in[d].astype(F32)
+        of = at_z(-d)
+        arrived(sum_in.at[of], sum_recv.at[of])
+        total = total + sum_in[of].astype(F32)
     out_ref[...] = total[:, :cols].astype(BF16)
+
+    for d in order:
+
+        @pl.when(at_y(-d) != t)
+        def _():
+            to_owner(d).wait_send()
 
     for copy in sent:
         copy.wait_send()
@@ -460,16 +563,20 @@
     latent_cache = jnp.swapaxes(latent_cache, 1, 2)
     out_proj = out_proj.T
     routes = routes.T
-    gain = norm_gain.reshape(1, cols)
     wide_cols = -(-cols // LANES) * LANES
     latent_dim = value_up.shape[1]
     slots = expert_slot.shape[0]
-    chunk = nx * block
     vmem = pl.BlockSpec(memory_space=pltpu.VMEM)
-    smem = pl.BlockSpec(memory_space=pltpu.SMEM)
     anywhere = pl.BlockSpec(memory_space=pltpu.HBM)
     sem = pltpu.SemaphoreType.DMA
     scratch = [
+        pltpu.SMEM(lengths.shape, jnp.int32),
+        pltpu.SMEM(expert_slot.shape, jnp.int32),
+        pltpu.VMEM(queries.shape, BF16),
+        pltpu.VMEM(residual_in.shape, BF16),
+        pltpu.VMEM(norm_gain.shape, BF16),
+        pltpu.VMEM(router.shape, BF16),
+        pltpu.VMEM(routes.shape, jnp.int32),
         pltpu.VMEM(latent_cache.shape, BF16),
         pltpu.VMEM(value_up.shape, BF16),
         pltpu.VMEM(out_proj.shape, BF16),
@@ -489,15 +596,16 @@
         pltpu.VMEM((2, nx, 8, wide_cols), F32),
         pltpu.VMEM((2, 2 * slots, wide_cols), BF16),
         pltpu.VMEM((nx, nz, block, 4 * units), BF16),
-        pltpu.VMEM((ny, nx, block, 4 * units), BF16),
-        pltpu.VMEM((ny, slots, LANES), BF16),
-        pltpu.VMEM((ny, slots, LANES), BF16),
-        pltpu.VMEM((2, ny, chunk, 2 * units), BF16),
-        pltpu.VMEM((ny, nx, block, wide_cols), BF16),
+        pltpu.VMEM((2, ny, 2, block, 4 * units), BF16),
+        pltpu.VMEM((2, ny, slots, LANES), BF16),
+        pltpu.VMEM((2, ny, slots, LANES), BF16),
+        pltpu.VMEM((2, 2, ny, 2 * block, 2 * units), BF16),
+        pltpu.VMEM((2, ny, 2, block, wide_cols), BF16),
         pltpu.VMEM((nx, ny, block, wide_cols), BF16),
         pltpu.VMEM((nz, block, wide_cols), BF16),
         pltpu.VMEM((nz, block, wide_cols), BF16),
         sem((4 + experts,)),
+        sem((7,)),
         sem((ny,)),
         sem((ny,)),
         sem((ny,)),
@@ -515,13 +623,13 @@
         sem((nx,)),
         sem((nx,)),
         sem((ny, nx)),
-        sem((ny,)),
-        sem((ny,)),
-        sem((ny,)),
-        sem((ny,)),
-        sem((ny,)),
-        sem((ny,)),
-        sem((ny,)),
+        sem((2, ny)),
+        sem((2, ny)),
+        sem((2, ny)),
+        sem((2, ny)),
+        sem((2, ny)),
+        sem((2, ny)),
+        sem((2, ny)),
         sem((nx, ny)),
         sem((nx, ny)),
         sem((nz,)),
@@ -530,7 +638,7 @@
     return pl.pallas_call(
         functools.partial(kernel, sizes, width),
         out_shape=jax.ShapeDtypeStruct((block, cols), BF16),
-        in_specs=[smem, smem, vmem, vmem, vmem, vmem, vmem] + [anywhere] * 5,
+        in_specs=[anywhere] * 12,
         out_specs=vmem,
         scratch_shapes=scratch,
         name="decode_layer",
@@ -542,7 +650,7 @@
         expert_slot,
         queries,
         residual_in,
-        gain,
+        norm_gain,
         router,
         routes,
         latent_cache,

time: 80.2 us -> 78.9 us (0.984)
  local copies, waits for them, and re-layouts: 2.58 us -> 1.32 us
    reshape x1 -> x0, local copies, waits for them, and re-layouts: 1.26 us -> none  [on_device(): gain = norm_gain.reshape(1, cols)]
where the time goes in v2:
time: 78.9 us; the launch traced here: 78.1 us
  Pallas kernels  76.7 us (97%)
  local copies, waits for them, and re-layouts  1.32 us (2%)
    pallas_call x1, Pallas kernels, on_device(): pl.pallas_call(functools.partial(kernel, sizes, width), out_shape=jax.Sha...  76.7 us

profile of v2, /device:TPU:1, one launch (start us, length us, event | category | flops | bytes accessed | tf_op | source)
XLA Modules:
  0.0 78.1 jit_solution(18154314996865187941)
XLA Ops:
  0.0 76.7 %decode_layer.1 = bf16[16,448]{1,0:T(8,128)(2,1)} custom-call(s32[8]{0:T(128)} %lengths_hbm.1, s32[16]{0:T(128)} %expert_slot_hbm.1, bf16[8,8,576]{2,1,0:T(8,128)(2,1)} %queries_hbm.1, bf16[16,448]{1,0:T(8,128)(2,1)} %residual_hbm.1, bf16[448]{0:T(512)(128)(2,1)} %gain_hbm.1, bf16[4,448]{1,0:T(4,128)(2,1)} %router_hbm.1, s32[8,16]{1,0:T(8,128)} %bitcast.9, ...), custom_call_target="tpu_custom_call" | custom-call | tf_op jit(solution)/shard_map/decode_layer/pallas_call | solution.py:638
  76.7 1.3 %copy.14 = bf16[16,448]{1,0:T(8,128)(2,1)} copy(bf16[16,448]{1,0:T(8,128)(2,1)} %decode_layer.1) | data formatting | bytes 28672

commit v3 on v2

--- a/solution.py
+++ b/solution.py
@@ -206,24 +206,27 @@
             ]
         )
     ]
-    for load in small[:2] + loads[:1] + small[2:] + loads[1:]:
+    for load in small[:2] + loads[:1]:
         load.start()
 
     score_scale = (VHEAD + ROPE) ** (-0.5)
-    for load in small[:2]:
+    for load in small[:2] + loads[:1]:
         load.wait()
-    loads[0].wait()
+    for load in loads[1:2] + small[2:] + loads[2:]:
+        load.start()
+    scores = []
+    positions = lax.broadcasted_iota(jnp.int32, (head_count, cache.shape[2]), 1)
     for n in range(seqs):
-        scores = dot(queries_ref[n], cache[n]) * score_scale
-        positions = lax.broadcasted_iota(jnp.int32, scores.shape, 1)
-        scores = jnp.where(positions < lengths_ref[n], scores, -1e30)
-        exps = jnp.exp(scores - jnp.max(scores, axis=1, keepdims=True))
-        probs = (exps / jnp.sum(exps, axis=1, keepdims=True)).astype(BF16)
-        of_seq = dot_nt(probs, cache[n, :latent_dim, :])
+        of_seq = dot(queries_ref[n], cache[n]) * score_scale
+        scores.append(jnp.where(positions < lengths_ref[n], of_seq, -1e30))
+    scores = jnp.concatenate(scores)
+    exps = jnp.exp(scores - jnp.max(scores, axis=1, keepdims=True))
+    probs = exps / jnp.sum(exps, axis=1, keepdims=True)
+    for n in range(seqs):
+        of_heads = slice(n * head_count, (n + 1) * head_count)
+        of_seq = dot_nt(probs[of_heads].astype(BF16), cache[n, :latent_dim, :])
         for q in range(latent_dim // LANES):
-            latent[q, n * head_count : (n + 1) * head_count, :] = of_seq[
-                :, q * LANES : (q + 1) * LANES
-            ]
+            latent[q, of_heads, :] = of_seq[:, q * LANES : (q + 1) * LANES]
     loads[1].wait()
     half = head_count // 2
     for low in range(half):
@@ -347,7 +350,7 @@
     rows[c, g, t, :, wide_cols - LANES :] = (total[:, wide_cols - LANES :] + marks).astype(BF16)
 
     mine = rows.at[c, g, t]
-    for d in far_zs:
+    for d in zs:
         send(mine, mine, row_z_send.at[d], row_z_recv.at[d], to_z(d))
     for a in (2, 1, 3):
         send(mine, mine, row_x_send.at[a, 0], row_x_recv.at[a], to_x(a))
@@ -473,21 +476,25 @@
             arrived(came, hid_recv.at[h, d])
             send(came, came, hid_core_send.at[h, d], hid_core_recv.at[h, d], partner)
 
-    def multiply_hidden(h, d):
-        of = at_y(-d)
-        arrived(hidden.at[h, other, of], hid_core_recv.at[h, d])
-        part = dot_nt(hidden[h, 0, of], down[:, :split])
-        part = part + dot_nt(hidden[h, 1, of], down[:, split:])
-        down_out[h, of, :, :, :cols] = part.astype(BF16).reshape(2, block, cols)
-        for place, code in enumerate(halves[h]):
-            if code:
-                send(
-                    down_out.at[h, of, place],
-                    down_in.at[code, of],
-                    down_send.at[code, d],
-                    down_recv.at[code, d],
-                    to_x(code),
-                )
+    def multiply_hidden(h, group):
+        for d in group:
+            arrived(hidden.at[h, other, at_y(-d)], hid_core_recv.at[h, d])
+        low_part = jnp.concatenate([hidden[h, 0, at_y(-d)] for d in group])
+        high_part = jnp.concatenate([hidden[h, 1, at_y(-d)] for d in group])
+        part = dot_nt(low_part, down[:, :split]) + dot_nt(high_part, down[:, split:])
+        part = part.astype(BF16).reshape(len(group), 2, block, cols)
+        for i, d in enumerate(group):
+            of = at_y(-d)
+            down_out[h, of, :, :, :cols] = part[i]
+            for place, code in enumerate(halves[h]):
+                if code:
+                    send(
+                        down_out.at[h, of, place],
+                        down_in.at[code, of],
+                        down_send.at[code, d],
+                        down_recv.at[code, d],
+                        to_x(code),
+                    )
 
     def to_owner(d):
         return pltpu.make_async_remote_copy(
@@ -512,16 +519,22 @@
             to_owner(d).start()
 
     order = [0] + ys
-    steps = [(h, d) for h in range(2) for d in order]
-    pass_hidden(*steps[0])
-    for i, (h, d) in enumerate(steps):
+    first = [order[i : i + 4] for i in range(0, ny, 4)]
+    second = [order[i : i + 2] for i in range(0, ny, 2)]
+    steps = [(0, group) for group in first] + [(1, group) for group in second]
+    for d in steps[0][1]:
+        pass_hidden(0, d)
+    for i, (h, group) in enumerate(steps):
         if i + 1 < len(steps):
-            pass_hidden(*steps[i + 1])
-        multiply_hidden(h, d)
-        if i - ny >= 2:
-            add_groups(order[i - ny - 2])
-    for d in order[max(ny - 2, 0) :]:
-        add_groups(d)
+            for d in steps[i + 1][1]:
+                pass_hidden(steps[i + 1][0], d)
+        multiply_hidden(h, group)
+        if i - len(first) >= 2:
+            for d in second[i - len(first) - 2]:
+                add_groups(d)
+    for group in second[-2:]:
+        for d in group:
+            add_groups(d)
     total = stream[...] + sum_out[t].astype(F32)
     for d in zs:
         of = at_z(-d)

time: 78.9 us -> 73 us (0.925)
  the two profiles are of different devices: /device:TPU:1 before, /device:TPU:40 now
where the time goes in v3:
time: 73 us; the launch traced here: 72.8 us
  Pallas kernels  71.5 us (98%)
  local copies, waits for them, and re-layouts  1.32 us (2%)
    pallas_call x1, Pallas kernels, on_device(): pl.pallas_call(functools.partial(kernel, sizes, width), out_shape=jax.Sha...  71.5 us

profile of v3, /device:TPU:40, one launch (start us, length us, event | category | flops | bytes accessed | tf_op | source)
XLA Modules:
  0.0 72.8 jit_solution(7176571875887092158)
XLA Ops:
  0.0 71.5 %decode_layer.1 = bf16[16,448]{1,0:T(8,128)(2,1)} custom-call(s32[8]{0:T(128)} %lengths_hbm.1, s32[16]{0:T(128)} %expert_slot_hbm.1, bf16[8,8,576]{2,1,0:T(8,128)(2,1)} %queries_hbm.1, bf16[16,448]{1,0:T(8,128)(2,1)} %residual_hbm.1, bf16[448]{0:T(512)(128)(2,1)} %gain_hbm.1, bf16[4,448]{1,0:T(4,128)(2,1)} %router_hbm.1, s32[8,16]{1,0:T(8,128)} %bitcast.9, ...), custom_call_target="tpu_custom_call" | custom-call | tf_op jit(solution)/shard_map/decode_layer/pallas_call | solution.py:651
  71.5 1.3 %copy.14 = bf16[16,448]{1,0:T(8,128)(2,1)} copy(bf16[16,448]{1,0:T(8,128)(2,1)} %decode_layer.1) | data formatting | bytes 28672

commit v4 on v3

--- a/solution.py
+++ b/solution.py
@@ -81,6 +81,7 @@
     sum_out,
     sum_in,
     load_sem,
+    cache_sem,
     small_sem,
     head_send,
     head_recv,
@@ -171,11 +172,6 @@
             device_id_type=MESH,
         ).wait_recv()
 
-    barrier = pltpu.get_barrier_semaphore()
-    peers = [partner] + [to_y(d) for d in ys] + [to_z(d) for d in zs] + [to_x(d) for d in xs]
-    for device in peers:
-        pl.semaphore_signal(barrier, inc=1, device_id=device, device_id_type=MESH)
-
     small = [
         pltpu.make_async_copy(src, dst, small_sem.at[i])
         for i, (src, dst) in enumerate(
@@ -195,7 +191,6 @@
         pltpu.make_async_copy(src, dst, load_sem.at[i])
         for i, (src, dst) in enumerate(
             [
-                (cache_hbm, cache),
                 (value_up_hbm, value_up),
                 (out_proj_hbm, out_proj),
                 (gate_up_hbm, gate_up),
@@ -206,19 +201,27 @@
             ]
         )
     ]
-    for load in small[:2] + loads[:1]:
+    cached = [
+        pltpu.make_async_copy(cache_hbm.at[n], cache.at[n], cache_sem.at[n]) for n in range(seqs)
+    ]
+    for load in small[:2] + cached + loads[:1]:
         load.start()
 
+    barrier = pltpu.get_barrier_semaphore()
+    peers = [partner] + [to_y(d) for d in ys] + [to_z(d) for d in zs] + [to_x(d) for d in xs]
+    for device in peers:
+        pl.semaphore_signal(barrier, inc=1, device_id=device, device_id_type=MESH)
+
     score_scale = (VHEAD + ROPE) ** (-0.5)
-    for load in small[:2] + loads[:1]:
+    for load in small[:2] + cached:
         load.wait()
-    for load in loads[1:2] + small[2:] + loads[2:]:
-        load.start()
     scores = []
     positions = lax.broadcasted_iota(jnp.int32, (head_count, cache.shape[2]), 1)
     for n in range(seqs):
         of_seq = dot(queries_ref[n], cache[n]) * score_scale
         scores.append(jnp.where(positions < lengths_ref[n], of_seq, -1e30))
+    for load in small[2:] + loads[1:]:
+        load.start()
     scores = jnp.concatenate(scores)
     exps = jnp.exp(scores - jnp.max(scores, axis=1, keepdims=True))
     probs = exps / jnp.sum(exps, axis=1, keepdims=True)
@@ -227,7 +230,7 @@
         of_seq = dot_nt(probs[of_heads].astype(BF16), cache[n, :latent_dim, :])
         for q in range(latent_dim // LANES):
             latent[q, of_heads, :] = of_seq[:, q * LANES : (q + 1) * LANES]
-    loads[1].wait()
+    loads[0].wait()
     half = head_count // 2
     for low in range(half):
         pair = []
@@ -267,7 +270,7 @@
     gain_column = dot_nt(
         identity.astype(BF16), jnp.broadcast_to(gain_row, (LANES, cols)).astype(BF16)
     )
-    loads[3].wait()
+    loads[2].wait()
     for dst, first in ((weights_out, other * 2), (weights.at[c], c * 2)):
         dst[cols:, :] = jnp.zeros((wide_cols - cols, dst.shape[1]), BF16)
         for j in range(2):
@@ -305,7 +308,7 @@
         came = heads.at[at_y(-d), c]
         arrived(came, head_recv.at[d])
         send(came, came, head_core_send.at[d], head_core_recv.at[d], partner)
-    loads[2].wait()
+    loads[1].wait()
     for d in [0] + ys:
         arrived(heads.at[at_y(-d), other], head_core_recv.at[d])
 
@@ -466,7 +469,7 @@
     down_out[:, :, :, :, wide_cols - LANES :] = jnp.zeros(down_out.shape[:4] + (LANES,), BF16)
     find_hidden(0)
     find_hidden(1)
-    for load in loads[4:]:
+    for load in loads[3:]:
         load.wait()
     split = down.shape[1] // 2
 
@@ -617,7 +620,8 @@
         pltpu.VMEM((nx, ny, block, wide_cols), BF16),
         pltpu.VMEM((nz, block, wide_cols), BF16),
         pltpu.VMEM((nz, block, wide_cols), BF16),
-        sem((4 + experts,)),
+        sem((3 + experts,)),
+        sem((seqs,)),
         sem((7,)),
         sem((ny,)),
         sem((ny,)),
@@ -650,7 +654,7 @@
     ]
     return pl.pallas_call(
         functools.partial(kernel, sizes, width),
-        out_shape=jax.ShapeDtypeStruct((block, cols), BF16),
+        out_shape=pltpu.VMEM((block, cols), BF16),
         in_specs=[anywhere] * 12,
         out_specs=vmem,
         scratch_shapes=scratch,

time: 73 us -> 70.6 us (0.967)
  the two profiles are of different devices: /device:TPU:40 before, /device:TPU:1 now
where the time goes in v4:
time: 70.6 us; the launch traced here: 70.4 us
  Pallas kernels  69.8 us (99%)
    pallas_call x1, Pallas kernels, on_device(): pl.pallas_call(functools.partial(kernel, sizes, width), out_shape=pltpu.V...  69.8 us

profile of v4, /device:TPU:1, one launch (start us, length us, event | category | flops | bytes accessed | tf_op | source)
XLA Modules:
  0.0 70.4 jit_solution(14332031999128797952)
XLA Ops:
  0.0 69.8 %decode_layer.1 = bf16[16,448]{1,0:T(8,128)(2,1)S(1)} custom-call(s32[8]{0:T(128)} %lengths_hbm.1, s32[16]{0:T(128)} %expert_slot_hbm.1, bf16[8,8,576]{2,1,0:T(8,128)(2,1)} %queries_hbm.1, bf16[16,448]{1,0:T(8,128)(2,1)} %residual_hbm.1, bf16[448]{0:T(512)(128)(2,1)} %gain_hbm.1, bf16[4,448]{1,0:T(4,128)(2,1)} %router_hbm.1, s32[8,16]{1,0:T(8,128)} %bitcast.9, ...), custom_call_target="tpu_custom_call" | custom-call | tf_op jit(solution)/shard_map/decode_layer/pallas_call | solution.py:655
  69.8 0.6 copy.14

commit v5 on v4

--- a/solution.py
+++ b/solution.py
@@ -148,7 +148,6 @@
         return (g, dp, at_z(d))
 
     partner = (g, y * 2 + other, t)
-    sent = []
 
     def send(src, dst, send_sem, recv_sem, device):
         copy = pltpu.make_async_remote_copy(
@@ -160,7 +159,6 @@
             device_id_type=MESH,
         )
         copy.start()
-        sent.append(copy)
 
     def arrived(dst, recv_sem):
         pltpu.make_async_remote_copy(
@@ -171,6 +169,16 @@
             device_id=partner,
             device_id_type=MESH,
         ).wait_recv()
+
+    def left(src, send_sem):
+        pltpu.make_async_remote_copy(
+            src_ref=src,
+            dst_ref=src,
+            send_sem=send_sem,
+            recv_sem=load_sem.at[0],
+            device_id=partner,
+            device_id_type=MESH,
+        ).wait_send()
 
     small = [
         pltpu.make_async_copy(src, dst, small_sem.at[i])
@@ -188,7 +196,7 @@
     ]
 
     loads = [
-        pltpu.make_async_copy(src, dst, load_sem.at[i])
+        pltpu.make_async_copy(src, dst, load_sem.at[min(i, 3)])
         for i, (src, dst) in enumerate(
             [
                 (value_up_hbm, value_up),
@@ -202,7 +210,7 @@
         )
     ]
     cached = [
-        pltpu.make_async_copy(cache_hbm.at[n], cache.at[n], cache_sem.at[n]) for n in range(seqs)
+        pltpu.make_async_copy(cache_hbm.at[n], cache.at[n], cache_sem) for n in range(seqs)
     ]
     for load in small[:2] + cached + loads[:1]:
         load.start()
@@ -213,7 +221,7 @@
         pl.semaphore_signal(barrier, inc=1, device_id=device, device_id_type=MESH)
 
     score_scale = (VHEAD + ROPE) ** (-0.5)
-    for load in small[:2] + cached:
+    for load in small[:2] + [pltpu.make_async_copy(cache_hbm, cache, cache_sem)]:
         load.wait()
     scores = []
     positions = lax.broadcasted_iota(jnp.int32, (head_count, cache.shape[2]), 1)
@@ -251,8 +259,8 @@
 
     mine = heads.at[y, c]
     for d in far_ys:
-        send(mine, mine, head_send.at[d], head_recv.at[d], to_y(d))
-    send(mine, mine, head_core_send.at[0], head_core_recv.at[0], partner)
+        send(mine, mine, head_send, head_recv.at[d], to_y(d))
+    send(mine, mine, head_core_send, head_core_recv, partner)
 
     for load in small[2:]:
         load.wait()
@@ -261,7 +269,7 @@
     router_all[c, g, :local_experts, :cols] = router_ref[...].astype(F32) * gain_row
     for d in xs:
         send(
-            router_all.at[c, g], router_all.at[c, g], router_send.at[d], router_recv.at[d], to_x(d)
+            router_all.at[c, g], router_all.at[c, g], router_send.at[1], router_recv.at[1], to_x(d)
         )
     identity = (
         lax.broadcasted_iota(jnp.int32, (cols, cols), 0)
@@ -307,10 +315,9 @@
     for d in ys:
         came = heads.at[at_y(-d), c]
         arrived(came, head_recv.at[d])
-        send(came, came, head_core_send.at[d], head_core_recv.at[d], partner)
+        send(came, came, head_core_send, head_core_recv, partner)
     loads[1].wait()
-    for d in [0] + ys:
-        arrived(heads.at[at_y(-d), other], head_core_recv.at[d])
+    arrived(heads.at[:, other], head_core_recv)
 
     gathered = heads[...].reshape(ny * 2 * 2 * seqs, half * VHEAD)
     low_part = dot_nt(gathered, out_proj[:, : half * VHEAD]).reshape(ny * 2, 2, seqs, cols)
@@ -318,10 +325,9 @@
     attn = (low_part[:, 0] + high_part[:, 1]).reshape(nz, block, cols)
     proj_out[:, :, :cols] = attn.astype(BF16)
     for d in far_zs:
-        send(proj_out.at[at_z(d)], proj_in.at[t], proj_send.at[d], proj_recv.at[d], to_z(d))
-
-    for d in xs:
-        arrived(router_all.at[c, at_x(d)], router_recv.at[d])
+        send(proj_out.at[at_z(d)], proj_in.at[t], proj_send, proj_recv, to_z(d))
+
+    arrived(router_all.at[c, pl.ds(1, nx - 1)], router_recv.at[1])
     send(router_all.at[c], router_all.at[c], router_send.at[0], router_recv.at[0], partner)
     arrived(weights.at[other], weight_recv)
     arrived(router_all.at[other], router_recv.at[0])
@@ -339,8 +345,8 @@
         router_rows[core, slots:] = squares_at.astype(F32).astype(BF16)
 
     total = residual[...] + proj_out[t].astype(F32)
+    arrived(proj_in.at[pl.ds(1, nz - 1)], proj_recv)
     for d in zs:
-        arrived(proj_in.at[at_z(-d)], proj_recv.at[d])
         total = total + proj_in[at_z(-d)].astype(F32)
     total = total.astype(BF16).astype(F32)
     stream[...] = total
@@ -354,19 +360,19 @@
 
     mine = rows.at[c, g, t]
     for d in zs:
-        send(mine, mine, row_z_send.at[d], row_z_recv.at[d], to_z(d))
+        send(mine, mine, row_z_send, row_z_recv.at[d], to_z(d))
     for a in (2, 1, 3):
-        send(mine, mine, row_x_send.at[a, 0], row_x_recv.at[a], to_x(a))
+        send(mine, mine, row_x_send.at[a], row_x_recv.at[a], to_x(a))
     for d in zs:
         came = rows.at[c, g, at_z(-d)]
         arrived(came, row_z_recv.at[d])
         for a in (2, 1, 3):
-            send(came, came, row_x_send.at[a, d], row_x_recv.at[a], to_x(a))
+            send(came, came, row_x_send.at[a], row_x_recv.at[a], to_x(a))
     def pass_rows(a):
         came = rows.at[c, at_x(a)]
         if a:
             arrived(came, row_x_recv.at[a])
-        send(came, came, row_core_send.at[a], row_core_recv.at[a], partner)
+        send(came, came, row_core_send, row_core_recv.at[a], partner)
 
     def multiply_rows(a):
         of = at_x(a)
@@ -379,8 +385,8 @@
             send(
                 part_out.at[of, at_y(d)],
                 part_in.at[of_half, y, place],
-                part_send.at[d, a],
-                part_recv.at[of_half, d],
+                part_send,
+                part_recv.at[of_half],
                 to_y(d),
             )
 
@@ -413,8 +419,8 @@
             send(
                 tail_out.at[h, at_y(d)],
                 tail_in.at[h, y],
-                tail_send.at[h, d],
-                tail_recv.at[h, d],
+                tail_send,
+                tail_recv.at[h],
                 to_y(d),
             )
 
@@ -436,13 +442,13 @@
     def find_hidden(h):
         tail = tail_out[h, y].astype(F32)
         total = jnp.concatenate([part_out[at_x(code), y] for code in halves[h]]).astype(F32)
+        arrived(tail_in.at[h, pl.ds(1, ny - 1)], tail_recv.at[h])
         for d in ys:
             of = at_y(-d)
-            arrived(tail_in.at[h, of], tail_recv.at[h, d])
             tail = tail + tail_in[h, of].astype(F32)
+        arrived(part_in.at[h, pl.ds(1, ny - 1)], part_recv.at[h])
         for d in ys:
             of = at_y(-d)
-            arrived(part_in.at[h, of], part_recv.at[h, d])
             total = total + part_in[h, of].reshape(total.shape).astype(F32)
         logits = dot_nt((across == down_at).astype(F32), tail, lax.Precision.HIGHEST)
         sums = dot_nt((across == down_at + chunk).astype(F32), tail, lax.Precision.HIGHEST)
@@ -463,25 +469,31 @@
             hidden[h, c, y, :, j * LANES : (j + 1) * LANES] = value.astype(BF16)
         mine = hidden.at[h, c, y]
         for d in ys:
-            send(mine, mine, hid_send.at[h, d], hid_recv.at[h, d], to_y(d))
-        send(mine, mine, hid_core_send.at[h, 0], hid_core_recv.at[h, 0], partner)
+            send(mine, mine, hid_send, hid_recv.at[h, d], to_y(d))
+        send(mine, mine, hid_core_send, hid_core_recv.at[group_of(h, 0)], partner)
 
     down_out[:, :, :, :, wide_cols - LANES :] = jnp.zeros(down_out.shape[:4] + (LANES,), BF16)
+    order = [0] + ys
+    first = [order[i : i + 4] for i in range(0, ny, 4)]
+    second = [order[i : i + 2] for i in range(0, ny, 2)]
+    steps = [(0, group) for group in first] + [(1, group) for group in second]
+
+    def group_of(h, d):
+        return [half == h and d in group for half, group in steps].index(True)
+
     find_hidden(0)
     find_hidden(1)
-    for load in loads[3:]:
-        load.wait()
+    pltpu.make_async_copy(down, down, load_sem.at[3]).wait()
     split = down.shape[1] // 2
 
     def pass_hidden(h, d):
         if d:
             came = hidden.at[h, c, at_y(-d)]
             arrived(came, hid_recv.at[h, d])
-            send(came, came, hid_core_send.at[h, d], hid_core_recv.at[h, d], partner)
+            send(came, came, hid_core_send, hid_core_recv.at[group_of(h, d)], partner)
 
     def multiply_hidden(h, group):
-        for d in group:
-            arrived(hidden.at[h, other, at_y(-d)], hid_core_recv.at[h, d])
+        arrived(hidden.at[h, other, pl.ds(0, len(group))], hid_core_recv.at[group_of(h, group[0])])
         low_part = jnp.concatenate([hidden[h, 0, at_y(-d)] for d in group])
         high_part = jnp.concatenate([hidden[h, 1, at_y(-d)] for d in group])
         part = dot_nt(low_part, down[:, :split]) + dot_nt(high_part, down[:, split:])
@@ -494,37 +506,25 @@
                     send(
                         down_out.at[h, of, place],
                         down_in.at[code, of],
-                        down_send.at[code, d],
-                        down_recv.at[code, d],
+                        down_send,
+                        down_recv.at[group_of(1, d) - len(first)],
                         to_x(code),
                     )
 
-    def to_owner(d):
-        return pltpu.make_async_remote_copy(
-            src_ref=sum_out.at[at_y(-d)],
-            dst_ref=sum_in.at[t],
-            send_sem=sum_send.at[d],
-            recv_sem=sum_recv.at[t],
-            device_id=(g, dp, at_y(-d)),
-            device_id_type=MESH,
-        )
-
-    def add_groups(d):
-        of = at_y(-d)
-        total = down_out[0, of, 0].astype(F32)
-        for a in (2, 1, 3):
-            arrived(down_in.at[a, of], down_recv.at[a, d])
-            total = total + down_in[a, of].astype(F32)
-        sum_out[of] = total.astype(BF16)
-
-        @pl.when(of != t)
-        def _():
-            to_owner(d).start()
-
-    order = [0] + ys
-    first = [order[i : i + 4] for i in range(0, ny, 4)]
-    second = [order[i : i + 2] for i in range(0, ny, 2)]
-    steps = [(0, group) for group in first] + [(1, group) for group in second]
+    def add_groups(group):
+        here = down_in.at[pl.ds(1, nx - 1), pl.ds(0, len(group))]
+        arrived(here, down_recv.at[second.index(group)])
+        for d in group:
+            of = at_y(-d)
+            total = down_out[0, of, 0].astype(F32)
+            for a in xs:
+                total = total + down_in[a, of].astype(F32)
+            sum_out[of] = total.astype(BF16)
+
+            @pl.when(of != t)
+            def _():
+                send(sum_out.at[of], sum_in.at[t], sum_send, sum_recv, (g, dp, of))
+
     for d in steps[0][1]:
         pass_hidden(0, d)
     for i, (h, group) in enumerate(steps):
@@ -533,26 +533,32 @@
                 pass_hidden(steps[i + 1][0], d)
         multiply_hidden(h, group)
         if i - len(first) >= 2:
-            for d in second[i - len(first) - 2]:
-                add_groups(d)
+            add_groups(second[i - len(first) - 2])
     for group in second[-2:]:
-        for d in group:
-            add_groups(d)
+        add_groups(group)
     total = stream[...] + sum_out[t].astype(F32)
+    arrived(sum_in.at[pl.ds(1, nz - 1)], sum_recv)
     for d in zs:
         of = at_z(-d)
-        arrived(sum_in.at[of], sum_recv.at[of])
         total = total + sum_in[of].astype(F32)
     out_ref[...] = total[:, :cols].astype(BF16)
 
-    for d in order:
-
-        @pl.when(at_y(-d) != t)
-        def _():
-            to_owner(d).wait_send()
-
-    for copy in sent:
-        copy.wait_send()
+    left(heads.at[pl.ds(1, ny - 1), c], head_send)
+    left(heads.at[:, c], head_core_send)
+    left(weights_out, weight_send)
+    left(router_all.at[c, pl.ds(1, nx - 1)], router_send.at[1])
+    left(router_all.at[c], router_send.at[0])
+    left(proj_out.at[pl.ds(1, nz - 1)], proj_send)
+    left(rows.at[c, g, pl.ds(1, nz - 1)], row_z_send)
+    for a in xs:
+        left(rows.at[c, g], row_x_send.at[a])
+    left(rows.at[c], row_core_send)
+    left(part_out.at[:, pl.ds(1, ny - 1)], part_send)
+    left(tail_out.at[:, pl.ds(1, ny - 1)], tail_send)
+    left(hidden.at[:, c, pl.ds(1, ny - 1)], hid_send)
+    left(hidden.at[:, c], hid_core_send)
+    left(down_in.at[pl.ds(1, nx - 1)], down_send)
+    left(sum_out.at[pl.ds(1, nz - 1)], sum_send)
 
 
 def on_device(sizes, width, *arrays):
@@ -620,37 +626,37 @@
         pltpu.VMEM((nx, ny, block, wide_cols), BF16),
         pltpu.VMEM((nz, block, wide_cols), BF16),
         pltpu.VMEM((nz, block, wide_cols), BF16),
-        sem((3 + experts,)),
-        sem((seqs,)),
+        sem((4,)),
+        sem,
         sem((7,)),
+        sem,
         sem((ny,)),
-        sem((ny,)),
-        sem((ny,)),
-        sem((ny,)),
-        sem,
-        sem,
+        sem,
+        sem,
+        sem,
+        sem,
+        sem((2,)),
+        sem((2,)),
+        sem,
+        sem,
+        sem,
+        sem((nz,)),
         sem((nx,)),
         sem((nx,)),
-        sem((nz,)),
-        sem((nz,)),
-        sem((nz,)),
-        sem((nz,)),
-        sem((nx, nz)),
+        sem,
         sem((nx,)),
-        sem((nx,)),
-        sem((nx,)),
-        sem((ny, nx)),
+        sem,
+        sem((2,)),
+        sem,
+        sem((2,)),
+        sem,
         sem((2, ny)),
-        sem((2, ny)),
-        sem((2, ny)),
-        sem((2, ny)),
-        sem((2, ny)),
-        sem((2, ny)),
-        sem((2, ny)),
-        sem((nx, ny)),
-        sem((nx, ny)),
-        sem((nz,)),
-        sem((nz,)),
+        sem,
+        sem((ny,)),
+        sem,
+        sem((ny,)),
+        sem,
+        sem,
     ]
     return pl.pallas_call(
         functools.partial(kernel, sizes, width),

time: 70.6 us -> 68.4 us (0.969)
  Pallas kernels: 69.8 us -> 67.6 us
    pallas_call x1, Pallas kernels: 69.8 us -> 67.6 us  [on_device(): pl.pallas_call(functools.partial(kernel, sizes, width), out_shape=pltpu.V...]
where the time goes in v5:
time: 68.4 us; the launch traced here: 68.3 us
  Pallas kernels  67.6 us (99%)
    pallas_call x1, Pallas kernels, on_device(): pl.pallas_call(functools.partial(kernel, sizes, width), out_shape=pltpu.V...  67.6 us

profile of v5, /device:TPU:1, one launch (start us, length us, event | category | flops | bytes accessed | tf_op | source)
XLA Modules:
  0.0 68.3 jit_solution(14138374761021544958)
XLA Ops:
  0.0 67.6 %decode_layer.1 = bf16[16,448]{1,0:T(8,128)(2,1)S(1)} custom-call(s32[8]{0:T(128)} %lengths_hbm.1, s32[16]{0:T(128)} %expert_slot_hbm.1, bf16[8,8,576]{2,1,0:T(8,128)(2,1)} %queries_hbm.1, bf16[16,448]{1,0:T(8,128)(2,1)} %residual_hbm.1, bf16[448]{0:T(512)(128)(2,1)} %gain_hbm.1, bf16[4,448]{1,0:T(4,128)(2,1)} %router_hbm.1, s32[8,16]{1,0:T(8,128)} %bitcast.9, ...), custom_call_target="tpu_custom_call" | custom-call | tf_op jit(solution)/shard_map/decode_layer/pallas_call | solution.py:661
  67.6 0.6 copy.14

commit v6 on v5

--- a/solution.py
+++ b/solution.py
@@ -216,7 +216,7 @@
         load.start()
 
     barrier = pltpu.get_barrier_semaphore()
-    peers = [partner] + [to_y(d) for d in ys] + [to_z(d) for d in zs] + [to_x(d) for d in xs]
+    peers = [to_y(d) for d in far_ys] + [to_z(d) for d in far_zs] + [to_x(d) for d in xs] + [partner]
     for device in peers:
         pl.semaphore_signal(barrier, inc=1, device_id=device, device_id_type=MESH)
 
@@ -652,9 +652,9 @@
         sem,
         sem((2, ny)),
         sem,
-        sem((ny,)),
-        sem,
-        sem((ny,)),
+        sem((max(ny - 2, 4),)),
+        sem,
+        sem((max(ny // 2, 1),)),
         sem,
         sem,
     ]

time: 68.4 us -> 68 us (level); the launches traced: 68.3 us -> 66.7 us
  Pallas kernels: 67.6 us -> 66.1 us
    pallas_call x1, Pallas kernels: 67.6 us -> 66.1 us  [on_device(): pl.pallas_call(functools.partial(kernel, sizes, width), out_shape=pltpu.V...]
where the time goes in v6:
time: 68 us; the launch traced here: 66.7 us
  Pallas kernels  66.1 us (97%)
    pallas_call x1, Pallas kernels, on_device(): pl.pallas_call(functools.partial(kernel, sizes, width), out_shape=pltpu.V...  66.1 us

profile of v6, /device:TPU:1, one launch (start us, length us, event | category | flops | bytes accessed | tf_op | source)
XLA Modules:
  0.0 66.7 jit_solution(308665628351365469)
XLA Ops:
  0.0 66.1 %decode_layer.1 = bf16[16,448]{1,0:T(8,128)(2,1)S(1)} custom-call(s32[8]{0:T(128)} %lengths_hbm.1, s32[16]{0:T(128)} %expert_slot_hbm.1, bf16[8,8,576]{2,1,0:T(8,128)(2,1)} %queries_hbm.1, bf16[16,448]{1,0:T(8,128)(2,1)} %residual_hbm.1, bf16[448]{0:T(512)(128)(2,1)} %gain_hbm.1, bf16[4,448]{1,0:T(4,128)(2,1)} %router_hbm.1, s32[8,16]{1,0:T(8,128)} %bitcast.9, ...), custom_call_target="tpu_custom_call" | custom-call | tf_op jit(solution)/shard_map/decode_layer/pallas_call | solution.py:661
  66.1 0.6 copy.14
